TPU v7x, 256 devices: a whole 4x4x8 slice. The times are simulated.
256 devices in a mesh: dp: 16 (over x, z_hi), expert: 16 (over y, z_lo, core).
Axes of the slice: x: 4, y: 4, z: 8 (z_hi: 4, z_lo: 2; z = z_hi * 2 + z_lo), core: 2. Of those that a mesh axis runs over, the one named last changes fastest.
Arguments:
- tokens: bfloat16 [32768, 2048], P(('dp', 'expert')), may hold values from -24 to 24
- grad_out: bfloat16 [32768, 2048], P(('dp', 'expert')), may hold values from -6 to 6
- expert_ids: int32 [32768, 6], P(('dp', 'expert')), may hold values from 0 to 63, all different within a row
- route_weights: float32 [32768, 6], P(('dp', 'expert')), may hold values from 0.05 to 0.5
- w_gate: bfloat16 [16, 2048, 768], P('expert'), may hold values from -0.125 to 0.125
- w_up: bfloat16 [16, 2048, 768], P('expert'), may hold values from -0.125 to 0.125
- w_down: bfloat16 [16, 2048, 768], P('expert'), may hold values from -0.21875 to 0.21875
Outputs:
- mixed: bfloat16 [32768, 2048], P(('dp', 'expert'))
- grad_tokens: bfloat16 [32768, 2048], P(('dp', 'expert'))
- grad_route: float32 [32768, 6], P(('dp', 'expert'))
- grad_gate: float32 [16, 2048, 768], P('expert', 'dp')
- grad_up: float32 [16, 2048, 768], P('expert', 'dp')
- grad_down: float32 [16, 2048, 768], P('expert', 'dp')
Inputs may be any that keep to these rules, and one draw needn't show every extreme that they name: `expert_ids`: each row names 6 different experts; only experts below 16 belong to this window.
All inputs are finite; a program needn't handle non-finite values.
Results may differ from a plain program's by a relative error of at most 0.033.
Values may be sent and summed in bfloat16 or wider, within the bound.
No kernel may reach another device: no remote copies, remote signals or barrier semaphores. Data moves between devices by JAX's collectives and lax.ppermute only.
A program may use at most 128 MiB of HBM per device.

v0:
```python
import jax
import jax.numpy as jnp
from jax import lax
from jax.sharding import PartitionSpec as P

CAP = 24


def slot_table(expert_ids, experts, capacity):
    pick_list = expert_ids.reshape(-1)
    expert_range = jnp.arange(experts, dtype=jnp.int32)
    matched = (pick_list[:, None] == expert_range[None, :]).astype(jnp.int32)
    earlier = jnp.cumsum(matched, axis=0) - matched
    position = jnp.sum(earlier * matched, axis=1)
    retained = (pick_list < experts) & (position < capacity)
    target = jnp.where(retained, pick_list * capacity + position, -1)
    return target.reshape(expert_ids.shape)


def on_device(tokens, grad_out, expert_ids, route_weights, w_gate, w_up, w_down):
    experts = lax.axis_size("expert")
    model_width = tokens.shape[1]
    capacity = CAP
    first_dims = (((0,), (0,)), ((), ()))
    contract_last = (((1,), (1,)), ((), ()))
    target = slot_table(expert_ids, experts, capacity)
    slot_ids = jnp.arange(experts * capacity, dtype=jnp.int32)
    matches = target[None, :, :] == slot_ids[:, None, None]
    row_ids = jnp.arange(tokens.shape[0], dtype=jnp.int32)
    source = jnp.sum(jnp.where(matches, row_ids[None, :, None], 0), axis=(1, 2))
    occupied = jnp.any(matches, axis=(1, 2))
    slot_weight = jnp.sum(jnp.where(matches, route_weights[None, :, :], 0.0), axis=(1, 2))
    picked_rows = tokens[source]
    send_rows = jnp.where(occupied[:, None], picked_rows, jnp.zeros_like(picked_rows))
    send_grads = (
        jnp.where(occupied, slot_weight, 0.0)[:, None] * grad_out[source].astype(jnp.float32)
    ).astype(jnp.bfloat16)
    slot_shape = (experts, capacity, model_width)
    arrived_rows, arrived_grads = (
        lax.all_to_all(
            send_rows.reshape(slot_shape), "expert", split_axis=0, concat_axis=0, tiled=True
        ),
        lax.all_to_all(
            send_grads.reshape(slot_shape), "expert", split_axis=0, concat_axis=0, tiled=True
        ),
    )
    inputs = arrived_rows.reshape(-1, model_width)
    upstream = arrived_grads.reshape(-1, model_width)
    gate_w = w_gate[0]
    up_w = w_up[0]
    down_w = w_down[0]
    hidden_width = gate_w.shape[1]
    gate_pre = jnp.dot(inputs, gate_w, preferred_element_type=jnp.float32)
    up_pre = jnp.dot(inputs, up_w, preferred_element_type=jnp.float32)
    hidden = (jax.nn.silu(gate_pre) * up_pre).astype(jnp.bfloat16)
    expert_out = lax.dot_general(
        hidden, down_w, contract_last, preferred_element_type=jnp.float32
    ).astype(jnp.bfloat16)
    d_hidden = jnp.dot(upstream, down_w, preferred_element_type=jnp.float32)
    sigmoid_gate = jax.nn.sigmoid(gate_pre)
    d_up = (d_hidden * gate_pre * sigmoid_gate).astype(jnp.bfloat16)
    d_gate = (d_hidden * up_pre * sigmoid_gate * (1.0 + gate_pre * (1.0 - sigmoid_gate))).astype(
        jnp.bfloat16
    )
    expert_dx = (
        lax.dot_general(d_gate, gate_w, contract_last, preferred_element_type=jnp.float32)
        + lax.dot_general(d_up, up_w, contract_last, preferred_element_type=jnp.float32)
    ).astype(jnp.bfloat16)
    returned_out, returned_dx = (
        lax.all_to_all(
            expert_out.reshape(slot_shape), "expert", split_axis=0, concat_axis=0, tiled=True
        ),
        lax.all_to_all(
            expert_dx.reshape(slot_shape), "expert", split_axis=0, concat_axis=0, tiled=True
        ),
    )
    stacked = lax.psum_scatter(
        jnp.concatenate(
            [
                jnp.concatenate(
                    [
                        lax.dot_general(
                            inputs, d_gate, first_dims, preferred_element_type=jnp.float32
                        ),
                        lax.dot_general(
                            inputs, d_up, first_dims, preferred_element_type=jnp.float32
                        ),
                    ],
                    axis=1,
                ),
                lax.dot_general(upstream, hidden, first_dims, preferred_element_type=jnp.float32),
            ],
            axis=1,
        ).astype(jnp.bfloat16),
        "dp",
        scatter_dimension=0,
        tiled=True,
    ).astype(jnp.float32)
    grad_gate = stacked[:, :hidden_width]
    grad_up = stacked[:, hidden_width : 2 * hidden_width]
    grad_down = stacked[:, 2 * hidden_width :]
    returned_out = returned_out.reshape(-1, model_width)
    returned_dx = returned_dx.reshape(-1, model_width)
    kept = target >= 0
    safe_slot = jnp.where(kept, target, 0)
    out_rows = returned_out[safe_slot].astype(jnp.float32)
    dx_rows = returned_dx[safe_slot].astype(jnp.float32)
    pick_weight = jnp.where(kept, route_weights, 0.0)
    mixed = jnp.sum(pick_weight[:, :, None] * out_rows, axis=1).astype(jnp.bfloat16)
    grad_tokens = jnp.sum(jnp.where(kept[:, :, None], dx_rows, 0.0), axis=1).astype(jnp.bfloat16)
    alignment = jnp.sum(out_rows * grad_out.astype(jnp.float32)[:, None, :], axis=2)
    grad_route = jnp.where(kept, alignment, 0.0)
    return (mixed, grad_tokens, grad_route, grad_gate[None], grad_up[None], grad_down[None])


def solution(mesh):
    placed = (
        P(("dp", "expert"), None),
        P(("dp", "expert"), None),
        P(("dp", "expert"), None),
        P(("dp", "expert"), None),
        P("expert", None, None),
        P("expert", None, None),
        P("expert", None, None),
    )
    return jax.shard_map(
        on_device,
        mesh=mesh,
        in_specs=placed,
        out_specs=(
            P(("dp", "expert"), None),
            P(("dp", "expert"), None),
            P(("dp", "expert"), None),
            P("expert", "dp", None),
            P("expert", "dp", None),
            P("expert", "dp", None),
        ),
        check_vma=False,
    )
```

profile of v0, /device:TPU:32, one launch (start us, length us, event | category | flops | bytes accessed | tf_op | source)
XLA Modules:
  0.0 285.6 jit_solution(3301339031622028751)
XLA Ops:
  7.2 0.9 copy.70
  8.1 0.1 eq.42
  8.3 0.1 eq.38
  8.4 1.7 reduce-window.6
  10.1 0.3 slice_reduce_fusion
  10.7 0.7 broadcast_select_fusion.3
  11.5 0.2 fusion.18
  11.7 0.9 select_reduce_fusion.1
  12.6 0.2 select_reduce_fusion.2
  13.0 6.2 %gather_fusion.2 = bf16[384,2048]{1,0:T(8,128)(2,1)} fusion(bf16[128,2048]{1,0:T(8,128)(2,1)} %param.8, s32[1024]{0:T(1024)S(1)} %pad_clamp_fusion.1), kind=kCustom, calls=%fused_computation.2 | custom fusion | bytes 3147264 | tf_op jit(solution)/shard_map/gather | solution.py:36
  19.2 2.9 %fusion = bf16[16,24,2048]{2,1,0:T(8,128)(2,1)} fusion(bf16[16,24,2048]{2,1,0:T(8,128)(2,1)} %bitcast.71, f32[16,24]{1,0:T(8,128)S(1)} %broadcast_select_fusion.1), kind=kLoop, calls=%fused_computation.12 | loop fusion | flops 2359296 | bytes 3147264 | tf_op jit(solution)/shard_map/convert_element_type | solution.py:37
  22.1 6.0 %all-to-all-start.2 = ((bf16[16,24,2048]{2,1,0:T(8,128)(2,1)}), bf16[16,24,2048]{2,1,0:T(8,128)(2,1)}, u32[]{:S(2)}, u32[]{:S(2)}) async-start(bf16[16,24,2048]{2,1,0:T(8,128)(2,1)} %fusion), calls=%async_computation.2 | async-start | bytes 3145728 | tf_op jit(solution)/shard_map/all_to_all | solution.py:43
  28.0 6.2 %gather_fusion = bf16[384,2048]{1,0:T(8,128)(2,1)} fusion(bf16[128,2048]{1,0:T(8,128)(2,1)} %param.7, s32[1024]{0:T(1024)S(1)} %pad_clamp_fusion.1), kind=kCustom, calls=%fused_computation | custom fusion | bytes 3147264 | tf_op jit(solution)/shard_map/gather | solution.py:33
  34.2 2.7 broadcast_select_fusion
  36.9 12.3 %all-to-all-done.2 = bf16[16,24,2048]{2,1,0:T(8,128)(2,1)} async-done(((bf16[16,24,2048]{2,1,0:T(8,128)(2,1)}), bf16[16,24,2048]{2,1,0:T(8,128)(2,1)}, u32[]{:S(2)}, u32[]{:S(2)}) %all-to-all-start.2) | async-done | bytes 1572896 | tf_op jit(solution)/shard_map/all_to_all | solution.py:43
  49.2 5.5 %all-to-all-start = ((bf16[16,24,2048]{2,1,0:T(8,128)(2,1)}), bf16[16,24,2048]{2,1,0:T(8,128)(2,1)}, u32[]{:S(2)}, u32[]{:S(2)}) async-start(bf16[16,24,2048]{2,1,0:T(8,128)(2,1)} %broadcast_select_fusion), calls=%async_computation | async-start | bytes 3145728 | tf_op jit(solution)/shard_map/all_to_all | solution.py:40
  54.7 0.2 reduce-scatter.4.cloned.1.call-start
  54.9 4.8 %fusion.1 = f32[384,768]{1,0:T(8,128)} fusion(bf16[384,2048]{1,0:T(8,128)(2,1)} %bitcast.9, bf16[1,2048,768]{2,1,0:T(8,128)(2,1)} %param.13), kind=kOutput, calls=%fused_computation.13 | convolution fusion | flops 1207959552 | bytes 5898240 | tf_op jit(solution)/shard_map/dot_general | solution.py:59
  59.7 16.1 %all-to-all-done = bf16[16,24,2048]{2,1,0:T(8,128)(2,1)} async-done(((bf16[16,24,2048]{2,1,0:T(8,128)(2,1)}), bf16[16,24,2048]{2,1,0:T(8,128)(2,1)}, u32[]{:S(2)}, u32[]{:S(2)}) %all-to-all-start) | async-done | bytes 1572896 | tf_op jit(solution)/shard_map/all_to_all | solution.py:40
  75.9 3.8 %fusion.7 = f32[384,768]{1,0:T(8,128)S(1)} fusion(bf16[384,2048]{1,0:T(8,128)(2,1)} %bitcast.2, bf16[1,2048,768]{2,1,0:T(8,128)(2,1)} %param.12), kind=kOutput, calls=%fused_computation.19 | convolution fusion | flops 1207959552 | bytes 5898240 | tf_op jit(solution)/shard_map/dot_general | solution.py:54
  79.7 3.2 %multiply_convert_fusion.1 = (bf16[384,768]{1,0:T(8,128)(2,1)S(1)}, bf16[384,768]{1,0:T(8,128)(2,1)S(1)}, bf16[384,768]{1,0:T(8,128)(2,1)S(1)}) fusion(f32[384,768]{1,0:T(8,128)S(1)} %copy-done.8, f32[384,768]{1,0:T(8,128)S(1)} %fusion.7, bf16[384,2048]{1,0:T(8,128)(2,1)} %bitcast.2, bf16[1,2048,768]{2,1,0:T(8,128)(2,1)S(1)} %copy-done), kind=kOutput, calls=%fused_computation.29 | convolution fusion | flops 1212678144 | bytes 8847360 | tf_op jit(solution)/shard_map/dot_general | solution.py:53
  83.0 3.9 %convolution_convert_fusion.1 = bf16[2048,768]{0,1:T(8,128)(2,1)S(1)} fusion(bf16[384,2048]{1,0:T(8,128)(2,1)} %bitcast.2, bf16[384,768]{1,0:T(8,128)(2,1)S(1)} %get-tuple-element.49), kind=kOutput, calls=%fused_computation.9 | convolution fusion | flops 1209532416 | bytes 5308416 | tf_op jit(solution)/shard_map/dot_general | solution.py:85
  86.9 3.3 %convolution_convert_fusion.2 = bf16[2048,768]{0,1:T(8,128)(2,1)S(1)} fusion(bf16[384,2048]{1,0:T(8,128)(2,1)} %bitcast.2, bf16[384,768]{1,0:T(8,128)(2,1)S(1)} %get-tuple-element.47), kind=kOutput, calls=%fused_computation.10 | convolution fusion | flops 1209532416 | bytes 5308416 | tf_op jit(solution)/shard_map/dot_general | solution.py:82
  90.2 3.3 %convolution_convert_fusion = bf16[2048,768]{0,1:T(8,128)(2,1)S(1)} fusion(bf16[384,2048]{1,0:T(8,128)(2,1)} %bitcast.9, bf16[384,768]{1,0:T(8,128)(2,1)S(1)} %get-tuple-element.48), kind=kOutput, calls=%fused_computation.8 | convolution fusion | flops 1209532416 | bytes 5308416 | tf_op jit(solution)/shard_map/dot_general | solution.py:91
  93.4 4.4 %pad_maximum_fusion = bf16[2048,2304]{0,1:T(8,128)(2,1)} fusion(bf16[2048,768]{0,1:T(8,128)(2,1)S(1)} %convolution_convert_fusion, bf16[2048,768]{0,1:T(8,128)(2,1)S(1)} %convolution_convert_fusion.1, bf16[2048,768]{0,1:T(8,128)(2,1)S(1)} %convolution_convert_fusion.2), kind=kLoop, calls=%fused_computation.4 | loop fusion | flops 28311552 | bytes 18874368 | tf_op jit(solution)/shard_map/concatenate | solution.py:78
  97.9 12.2 %copy.82 = bf16[2048,2304]{1,0:T(8,128)(2,1)} copy(bf16[2048,2304]{0,1:T(8,128)(2,1)} %pad_maximum_fusion) | data formatting | bytes 18874368
  110.1 3.5 %fusion.5 = f32[384,2048]{1,0:T(8,128)S(1)} fusion(bf16[384,768]{1,0:T(8,128)(2,1)} %copy-done.7, bf16[1,2048,768]{2,1,0:T(8,128)(2,1)} %param.12), kind=kOutput, calls=%fused_computation.17 | convolution fusion | flops 1207959552 | bytes 6881280 | tf_op jit(solution)/shard_map/dot_general | solution.py:67
  113.6 2.6 add_convert_fusion
  116.2 5.0 %all-to-all-start.3 = ((bf16[16,24,2048]{2,1,0:T(8,128)(2,1)}), bf16[16,24,2048]{2,1,0:T(8,128)(2,1)S(1)}, u32[]{:S(2)}, u32[]{:S(2)}) async-start(bf16[16,24,2048]{2,1,0:T(8,128)(2,1)} %bitcast.74), calls=%async_computation.3 | async-start | bytes 3145728 | tf_op jit(solution)/shard_map/all_to_all | solution.py:73
  121.2 4.5 %fusion.15 = bf16[384,2048]{1,0:T(8,128)(2,1)} fusion(bf16[384,768]{1,0:T(8,128)(2,1)S(1)} %copy-done.6, bf16[1,2048,768]{2,1,0:T(8,128)(2,1)} %param.13), kind=kOutput, calls=%fused_computation.26 | convolution fusion | flops 1208745984 | bytes 5308416 | tf_op jit(solution)/shard_map/dot_general | solution.py:56
  125.7 46.6 %all-to-all-done.3 = bf16[16,24,2048]{2,1,0:T(8,128)(2,1)S(1)} async-done(((bf16[16,24,2048]{2,1,0:T(8,128)(2,1)}), bf16[16,24,2048]{2,1,0:T(8,128)(2,1)S(1)}, u32[]{:S(2)}, u32[]{:S(2)}) %all-to-all-start.3) | async-done | bytes 1572896 | tf_op jit(solution)/shard_map/all_to_all | solution.py:73
  172.3 9.0 %all-to-all-start.1 = ((bf16[16,24,2048]{2,1,0:T(8,128)(2,1)}), bf16[16,24,2048]{2,1,0:T(8,128)(2,1)S(1)}, u32[]{:S(2)}, u32[]{:S(2)}) async-start(bf16[16,24,2048]{2,1,0:T(8,128)(2,1)} %bitcast.73), calls=%async_computation.1 | async-start | bytes 3145728 | tf_op jit(solution)/shard_map/all_to_all | solution.py:70
  181.3 2.2 convert_element_type.66
  183.5 0.1 copy.77
  183.8 0.1 reshape.120
  184.1 4.3 %gather_fusion.3 = bf16[768,2048]{1,0:T(8,128)(2,1)} fusion(bf16[384,2048]{1,0:T(8,128)(2,1)S(1)} %bitcast.69, s32[1024]{0:T(1024)S(1)} %pad_clamp_fusion), kind=kCustom, calls=%fused_computation.3 | custom fusion | bytes 6294528 | tf_op jit(solution)/shard_map/gather | solution.py:107
  188.4 6.5 %reshape.147 = f32[128,6,2048]{2,1,0:T(8,128)} reshape(bf16[768,2048]{1,0:T(8,128)(2,1)} %gather_fusion.3) | data formatting | bytes 9437184 | tf_op jit(solution)/shard_map/convert_element_type | solution.py:107
  194.9 39.7 %all-to-all-done.1 = bf16[16,24,2048]{2,1,0:T(8,128)(2,1)S(1)} async-done(((bf16[16,24,2048]{2,1,0:T(8,128)(2,1)}), bf16[16,24,2048]{2,1,0:T(8,128)(2,1)S(1)}, u32[]{:S(2)}, u32[]{:S(2)}) %all-to-all-start.1) | async-done | bytes 1572896 | tf_op jit(solution)/shard_map/all_to_all | solution.py:70
  234.6 4.2 %gather_fusion.1 = bf16[768,2048]{1,0:T(8,128)(2,1)} fusion(bf16[384,2048]{1,0:T(8,128)(2,1)S(1)} %bitcast.70, s32[1024]{0:T(1024)S(1)} %pad_clamp_fusion), kind=kCustom, calls=%fused_computation.1 | custom fusion | bytes 6294528 | tf_op jit(solution)/shard_map/gather | solution.py:106
  238.8 6.7 %reshape.146 = f32[128,6,2048]{2,1,0:T(8,128)} reshape(bf16[768,2048]{1,0:T(8,128)(2,1)} %gather_fusion.1) | data formatting | bytes 9437184 | tf_op jit(solution)/shard_map/convert_element_type | solution.py:106
  245.5 12.7 %multiply_reduce_fusion = (f32[128,6]{1,0:T(8,128)S(1)}, bf16[128,2048]{1,0:T(8,128)(2,1)}, bf16[128,2048]{1,0:T(8,128)(2,1)}) fusion(f32[128,6,2048]{2,1,0:T(8,128)} %reshape.146, f32[128,2048]{1,0:T(8,128)S(1)} %copy-done.2, f32[128,6]{1,0:T(8,128)S(1)} %copy.75, f32[128,6,2048]{2,1,0:T(8,128)} %reshape.147, pred[128,6]{1,0:T(8,128)(4,1)S(1)} %copy.77), kind=kLoop, calls=%fused_computation.5 | loop fusion | flops 8912128 | bytes 14686976 | tf_op jit(solution)/shard_map/reduce_sum | solution.py:111
  258.3 0.6 broadcast_select_fusion.2
  259.0 12.4 %reduce-scatter.4.cloned.1.call-done = bf16[128,2304]{1,0:T(8,128)(2,1)} async-done(((bf16[2048,2304]{1,0:T(8,128)(2,1)}), bf16[128,2304]{1,0:T(8,128)(2,1)}) %reduce-scatter.4.cloned.1.call-update) | async-done | bytes 589840
  271.4 1.4 copy.83
  272.8 1.0 slice_bitcast_fusion
  273.8 2.2 copy.79
  276.0 1.9 copy.80
  277.9 0.9 copy.81
  (35 shorter events, 1.0 us)
Async XLA Ops:
  7.2 72.6 %copy-start = (bf16[1,2048,768]{2,1,0:T(8,128)(2,1)S(1)}, bf16[1,2048,768]{2,1,0:T(8,128)(2,1)}, u32[]{:S(2)}) copy-start(bf16[1,2048,768]{2,1,0:T(8,128)(2,1)} %param.11) | copy-start | bytes 9437188
  22.1 27.1 %all-to-all-start.2 = ((bf16[16,24,2048]{2,1,0:T(8,128)(2,1)}), bf16[16,24,2048]{2,1,0:T(8,128)(2,1)}, u32[]{:S(2)}, u32[]{:S(2)}) async-start(bf16[16,24,2048]{2,1,0:T(8,128)(2,1)} %fusion), calls=%async_computation.2 | async-start | bytes 3145728 | tf_op jit(solution)/shard_map/all_to_all | solution.py:43
  49.2 26.7 %all-to-all-start = ((bf16[16,24,2048]{2,1,0:T(8,128)(2,1)}), bf16[16,24,2048]{2,1,0:T(8,128)(2,1)}, u32[]{:S(2)}, u32[]{:S(2)}) async-start(bf16[16,24,2048]{2,1,0:T(8,128)(2,1)} %broadcast_select_fusion), calls=%async_computation | async-start | bytes 3145728 | tf_op jit(solution)/shard_map/all_to_all | solution.py:40
  54.7 216.7 %reduce-scatter.4.cloned.1.call-start = ((), (), s32[]{:S(2)}) async-start(), calls=%async_computation.5 | async-start | bytes 10027008
  75.9 3.9 %copy-start.8 = (f32[384,768]{1,0:T(8,128)S(1)}, f32[384,768]{1,0:T(8,128)}, u32[]{:S(2)}) copy-start(f32[384,768]{1,0:T(8,128)} %fusion.1) | copy-start | bytes 3538948
  83.0 3.9 %copy-start.7 = (bf16[384,768]{1,0:T(8,128)(2,1)}, bf16[384,768]{1,0:T(8,128)(2,1)S(1)}, u32[]{:S(2)}) copy-start(bf16[384,768]{1,0:T(8,128)(2,1)S(1)} %get-tuple-element.49) | copy-start | bytes 1769476
  83.0 3.9 %copy-start.3 = (bf16[384,768]{1,0:T(8,128)(2,1)}, bf16[384,768]{1,0:T(8,128)(2,1)S(1)}, u32[]{:S(2)}) copy-start(bf16[384,768]{1,0:T(8,128)(2,1)S(1)} %get-tuple-element.47) | copy-start | bytes 1769476
  83.0 7.2 %copy-start.5 = (bf16[384,768]{1,0:T(8,128)(2,1)}, bf16[384,768]{1,0:T(8,128)(2,1)S(1)}, u32[]{:S(2)}) copy-start(bf16[384,768]{1,0:T(8,128)(2,1)S(1)} %get-tuple-element.48) | copy-start | bytes 1769476
  110.1 3.6 %copy-start.4 = (bf16[384,768]{1,0:T(8,128)(2,1)S(1)}, bf16[384,768]{1,0:T(8,128)(2,1)}, u32[]{:S(2)}) copy-start(bf16[384,768]{1,0:T(8,128)(2,1)} %copy-done.3) | copy-start | bytes 1769476
  116.2 5.0 %copy-start.6 = (bf16[384,768]{1,0:T(8,128)(2,1)S(1)}, bf16[384,768]{1,0:T(8,128)(2,1)}, u32[]{:S(2)}) copy-start(bf16[384,768]{1,0:T(8,128)(2,1)} %copy-done.5) | copy-start | bytes 1769476
  116.2 56.1 %all-to-all-start.3 = ((bf16[16,24,2048]{2,1,0:T(8,128)(2,1)}), bf16[16,24,2048]{2,1,0:T(8,128)(2,1)S(1)}, u32[]{:S(2)}, u32[]{:S(2)}) async-start(bf16[16,24,2048]{2,1,0:T(8,128)(2,1)} %bitcast.74), calls=%async_computation.3 | async-start | bytes 3145728 | tf_op jit(solution)/shard_map/all_to_all | solution.py:73
  172.3 62.3 %all-to-all-start.1 = ((bf16[16,24,2048]{2,1,0:T(8,128)(2,1)}), bf16[16,24,2048]{2,1,0:T(8,128)(2,1)S(1)}, u32[]{:S(2)}, u32[]{:S(2)}) async-start(bf16[16,24,2048]{2,1,0:T(8,128)(2,1)} %bitcast.73), calls=%async_computation.1 | async-start | bytes 3145728 | tf_op jit(solution)/shard_map/all_to_all | solution.py:70
  238.8 6.7 %copy-start.2 = (f32[128,2048]{1,0:T(8,128)S(1)}, f32[128,2048]{1,0:T(8,128)}, u32[]{:S(2)}) copy-start(f32[128,2048]{1,0:T(8,128)} %convert_element_type.66) | copy-start | bytes 3145732
  272.8 6.0 %copy-start.1 = (bf16[1,2048,768]{2,1,0:T(8,128)(2,1)S(1)}, bf16[1,2048,768]{2,1,0:T(8,128)(2,1)}, u32[]{:S(2)}) copy-start(bf16[1,2048,768]{2,1,0:T(8,128)(2,1)} %param.11) | copy-start | bytes 9437188
Sparse Core Ops, SparseCore 0:
  110.2 161.1 reduce-scatter.3
where the time goes:
time: 288 us; the launch traced here: 286 us
  waiting for transfers between devices  127 us (44%)
  local copies, waits for them, and re-layouts  56 us (19%)
  matrix products  32.8 us (11%)
  other arithmetic  29.6 us (10%)
  starting transfers between devices  25.7 us (9%)
  between operations  14.3 us (5%)
    all_to_all x1, waiting for transfers between devices, on_device(): lax.all_to_all(expert_dx.reshape(slot_shape), 'expert', split_axis=0, con...  46.6 us
    all_to_all x1, waiting for transfers between devices, on_device(): lax.all_to_all(expert_out.reshape(slot_shape), 'expert', split_axis=0, co...  39.7 us
    unnamed x24, local copies, waits for them, and re-layouts  19.5 us
    all_to_all x1, waiting for transfers between devices, on_device(): lax.all_to_all(send_rows.reshape(slot_shape), 'expert', split_axis=0, con...  16.1 us
    reduce_sum x1, other arithmetic, on_device(): jnp.sum(out_rows * grad_out.astype(jnp.float32)[:, None, :], axis=2)  12.7 us
    unnamed x2, waiting for transfers between devices  12.4 us
    all_to_all x1, waiting for transfers between devices, on_device(): lax.all_to_all(send_grads.reshape(slot_shape), 'expert', split_axis=0, co...  12.3 us
    all_to_all x1, starting transfers between devices, on_device(): lax.all_to_all(expert_out.reshape(slot_shape), 'expert', split_axis=0, co...  8.99 us
  transfers between devices with their start and end apart: 5, of which 5 were waited for; matrix products, arithmetic and copies ran while one was open for 22% of the time, Pallas kernels for 0%

commit v1 on v0

v1 whole, which is shorter than its diff:
```python
import functools

import jax
import jax.numpy as jnp
from jax import lax
from jax.experimental import pallas as pl
from jax.experimental.pallas import tpu as pltpu
from jax.sharding import PartitionSpec as P

CAP = 24
EXPERTS = 16
SLOTS = EXPERTS * CAP
ROWS = 128
TOP = 6
D = 2048
FF = 768
RING = 4
MIB = 1024 * 1024
F32 = jnp.float32
BF16 = jnp.bfloat16
ALL = ("dp", "expert")


def ring_perm(axis):
    pairs = []
    for dp in range(16):
        x, z = divmod(dp, RING)
        for expert in range(16):
            step = 1 if expert % 2 == 0 else -1
            if axis == "x":
                to = ((x + step) % RING) * RING + z
            else:
                to = x * RING + (z + step) % RING
            pairs.append((dp * 16 + expert, to * 16 + expert))
    return pairs


def dot(a, b, contract):
    return lax.dot_general(a, b, ((contract[:1], contract[1:]), ((), ())), preferred_element_type=F32)


def place_kernel(ids_ref, weights_ref, tokens_ref, grads_ref, send_ref, target_ref):
    ids = ids_ref[...]
    weights = weights_ref[...]
    expert = lax.broadcasted_iota(jnp.int32, (EXPERTS, ROWS), 0)
    picked = jnp.zeros((EXPERTS, ROWS), F32)
    for k in range(TOP):
        picked = picked + jnp.where(ids[k : k + 1, :] == expert, 1.0, 0.0)
    earlier = lax.broadcasted_iota(jnp.int32, (ROWS, ROWS), 0) < lax.broadcasted_iota(
        jnp.int32, (ROWS, ROWS), 1
    )
    position = jnp.dot(
        picked.astype(BF16),
        jnp.where(earlier, 1.0, 0.0).astype(BF16),
        preferred_element_type=F32,
    )
    slot = lax.broadcasted_iota(jnp.int32, (SLOTS, ROWS), 0)
    chosen = jnp.zeros((SLOTS, ROWS), F32)
    scale = jnp.zeros((SLOTS, ROWS), F32)
    for k in range(TOP):
        pick = ids[k : k + 1, :]
        own = jnp.sum(jnp.where(pick == expert, position, 0.0), axis=0, keepdims=True)
        place = own.astype(jnp.int32)
        target = jnp.where((pick < EXPERTS) & (place < CAP), pick * CAP + place, -1)
        target_ref[k : k + 1, :] = target
        here = target == slot
        chosen = chosen + jnp.where(here, 1.0, 0.0)
        scale = scale + jnp.where(here, weights[k : k + 1, :], 0.0)
    chosen = chosen.astype(BF16)
    slot_scale = jnp.sum(scale, axis=1, keepdims=True)
    send_ref[:, :D] = jnp.dot(chosen, tokens_ref[...], preferred_element_type=F32).astype(BF16)
    send_ref[:, D:] = (
        slot_scale * jnp.dot(chosen, grads_ref[...], preferred_element_type=F32)
    ).astype(BF16)


def place(ids, weights, tokens, grads):
    return pl.pallas_call(
        place_kernel,
        out_shape=(
            jax.ShapeDtypeStruct((SLOTS, 2 * D), BF16),
            jax.ShapeDtypeStruct((TOP, ROWS), jnp.int32),
        ),
        compiler_params=pltpu.CompilerParams(vmem_limit_bytes=40 * MIB),
        cost_estimate=pl.CostEstimate(flops=4 * 10**8, bytes_accessed=5 * MIB, transcendentals=0),
        name="place_rows",
    )(ids, weights, tokens, grads)


def hidden_kernel(rows_ref, gate_ref, up_ref, down_ref, hidden_ref, d_gate_ref, d_up_ref):
    inputs = rows_ref[:, :D]
    gate_pre = jnp.dot(inputs, gate_ref[...], preferred_element_type=F32)
    up_pre = jnp.dot(inputs, up_ref[...], preferred_element_type=F32)
    d_hidden = jnp.dot(rows_ref[:, D:], down_ref[...], preferred_element_type=F32)
    sigmoid = jax.nn.sigmoid(gate_pre)
    silu = gate_pre * sigmoid
    hidden_ref[...] = (silu * up_pre).astype(BF16)
    d_up_ref[...] = (d_hidden * silu).astype(BF16)
    d_gate_ref[...] = (d_hidden * up_pre * sigmoid * (1.0 + gate_pre * (1.0 - sigmoid))).astype(BF16)


def hidden_pass(rows, gate_w, up_w, down_w):
    tile = 256
    weight = pl.BlockSpec((D, tile), lambda i: (0, i))
    out = pl.BlockSpec((SLOTS, tile), lambda i: (0, i))
    return pl.pallas_call(
        hidden_kernel,
        grid=(FF // tile,),
        in_specs=[pl.BlockSpec((SLOTS, 2 * D), lambda i: (0, 0)), weight, weight, weight],
        out_specs=[out] * 3,
        out_shape=[jax.ShapeDtypeStruct((SLOTS, FF), BF16)] * 3,
        compiler_params=pltpu.CompilerParams(vmem_limit_bytes=40 * MIB),
        cost_estimate=pl.CostEstimate(
            flops=6 * SLOTS * D * FF, bytes_accessed=14 * MIB, transcendentals=SLOTS * FF
        ),
        name="hidden_pass",
    )(rows, gate_w, up_w, down_w)


OUT_TILE = 512


def back_kernel(hidden_ref, d_gate_ref, d_up_ref, gate_ref, up_ref, down_ref, out_ref):
    out_ref[:, :OUT_TILE] = dot(hidden_ref[...], down_ref[...], (1, 1)).astype(BF16)
    out_ref[:, OUT_TILE:] = (
        dot(d_gate_ref[...], gate_ref[...], (1, 1)) + dot(d_up_ref[...], up_ref[...], (1, 1))
    ).astype(BF16)


def back_pass(hidden, d_gate, d_up, gate_w, up_w, down_w):
    act = pl.BlockSpec((SLOTS, FF), lambda i: (0, 0))
    weight = pl.BlockSpec((OUT_TILE, FF), lambda i: (i, 0))
    return pl.pallas_call(
        back_kernel,
        grid=(D // OUT_TILE,),
        in_specs=[act, act, act, weight, weight, weight],
        out_specs=pl.BlockSpec((SLOTS, 2 * OUT_TILE), lambda i: (0, i)),
        out_shape=jax.ShapeDtypeStruct((SLOTS, 2 * D), BF16),
        compiler_params=pltpu.CompilerParams(vmem_limit_bytes=40 * MIB),
        cost_estimate=pl.CostEstimate(
            flops=6 * SLOTS * D * FF, bytes_accessed=14 * MIB, transcendentals=0
        ),
        name="back_pass",
    )(hidden, d_gate, d_up, gate_w, up_w, down_w)


def partial_kernel(at_ref, lhs_ref, rhs_ref, *refs):
    total = dot(lhs_ref[...], rhs_ref[...], (0, 0))
    if len(refs) == 2:
        total = total + refs[0][...].astype(F32)
    refs[-1][...] = total.astype(BF16)


def partial_last_kernel(at_ref, lhs_ref, rhs_ref, got_ref, *out_refs):
    for i, out_ref in enumerate(out_refs):
        start = pl.multiple_of(at_ref[1 + i] * ROWS, ROWS)
        total = dot(lhs_ref[:, pl.ds(start, ROWS)], rhs_ref[...], (0, 0))
        total = total + got_ref[pl.ds(start, ROWS), :].astype(F32)
        out_ref[...] = total.astype(BF16)


def partial_sum(at, rows, half, grads, column, width, got, last):
    chunk = D // RING
    in_specs = [
        pl.BlockSpec((SLOTS, chunk), lambda i, at: (0, half * RING + at[0])),
        pl.BlockSpec((SLOTS, width), lambda i, at: (0, column)),
    ]
    args = [rows, grads]
    whole = pl.BlockSpec((chunk, width), lambda i, at: (0, 0))
    if got is not None:
        in_specs.append(whole)
        args.append(got)
    if last:
        out_specs = [pl.BlockSpec((ROWS, width), lambda i, at: (0, 0))] * RING
        out_shape = [jax.ShapeDtypeStruct((ROWS, width), BF16)] * RING
    else:
        out_specs = whole
        out_shape = jax.ShapeDtypeStruct((chunk, width), BF16)
    return pl.pallas_call(
        partial_last_kernel if last else partial_kernel,
        grid_spec=pltpu.PrefetchScalarGridSpec(
            num_scalar_prefetch=1, grid=(1,), in_specs=in_specs, out_specs=out_specs
        ),
        out_shape=out_shape,
        compiler_params=pltpu.CompilerParams(vmem_limit_bytes=24 * MIB),
        cost_estimate=pl.CostEstimate(
            flops=2 * SLOTS * chunk * width, bytes_accessed=3 * MIB, transcendentals=0
        ),
        name="partial_last" if last else "partial_sum",
    )(at, *args)


def combine_kernel(target_ref, weights_ref, back_ref, grads_ref, mixed_ref, d_tokens_ref, d_route_ref):
    weights = weights_ref[...]
    slot = lax.broadcasted_iota(jnp.int32, (SLOTS, ROWS), 0)
    align = jnp.zeros((SLOTS, ROWS), F32)
    tiles = D // OUT_TILE
    for i in range(tiles):
        out = back_ref[:, 2 * i * OUT_TILE : (2 * i + 1) * OUT_TILE]
        align = align + dot(out, grads_ref[:, i * OUT_TILE : (i + 1) * OUT_TILE], (1, 1))
    chosen = jnp.zeros((SLOTS, ROWS), F32)
    scale = jnp.zeros((SLOTS, ROWS), F32)
    for k in range(TOP):
        here = target_ref[k : k + 1, :] == slot
        chosen = chosen + jnp.where(here, 1.0, 0.0)
        scale = scale + jnp.where(here, weights[k : k + 1, :], 0.0)
        d_route_ref[k : k + 1, :] = jnp.sum(jnp.where(here, align, 0.0), axis=0, keepdims=True)
    chosen = chosen.astype(BF16)
    high = scale.astype(BF16)
    low = (scale - high.astype(F32)).astype(BF16)
    for i in range(tiles):
        out = back_ref[:, 2 * i * OUT_TILE : (2 * i + 1) * OUT_TILE]
        d_in = back_ref[:, (2 * i + 1) * OUT_TILE : (2 * i + 2) * OUT_TILE]
        at = slice(i * OUT_TILE, (i + 1) * OUT_TILE)
        mixed_ref[:, at] = (dot(high, out, (0, 0)) + dot(low, out, (0, 0))).astype(BF16)
        d_tokens_ref[:, at] = dot(chosen, d_in, (0, 0)).astype(BF16)


def combine(target, weights, back, grads):
    return pl.pallas_call(
        combine_kernel,
        out_shape=(
            jax.ShapeDtypeStruct((ROWS, D), BF16),
            jax.ShapeDtypeStruct((ROWS, D), BF16),
            jax.ShapeDtypeStruct((TOP, ROWS), F32),
        ),
        compiler_params=pltpu.CompilerParams(vmem_limit_bytes=40 * MIB),
        cost_estimate=pl.CostEstimate(flops=10**9, bytes_accessed=6 * MIB, transcendentals=0),
        name="combine_rows",
    )(target, weights, back, grads)


def on_device(tokens, grad_out, expert_ids, route_weights, w_gate, w_up, w_down):
    x, z = lax.axis_index("dp") // RING, lax.axis_index("dp") % RING
    step = 1 - 2 * (lax.axis_index("expert") % 2)
    x_at = [(x - (i + 1) * step) % RING for i in range(RING)]
    z_at = [(z - (i + 1) * step) % RING for i in range(RING)]
    order = [jnp.stack([at, *z_at]).astype(jnp.int32) for at in x_at]
    x_perm, z_perm = ring_perm("x"), ring_perm("z")
    gate_w, up_w, down_w = w_gate[0], w_up[0], w_down[0]
    ids, weights = expert_ids.T, route_weights.T

    def exchange(buffer):
        buffer = buffer.reshape(EXPERTS, CAP, 2 * D)
        buffer = lax.all_to_all(buffer, "expert", split_axis=0, concat_axis=0, tiled=True)
        return buffer.reshape(SLOTS, 2 * D)

    send, target = place(ids, weights, tokens, grad_out)
    rows = exchange(send)
    hidden, d_gate, d_up = hidden_pass(rows, gate_w, up_w, down_w)

    def x_ring(half, grads, column, width):
        got = None
        for i in range(RING):
            total = partial_sum(order[i], rows, half, grads, column, width, got, i == RING - 1)
            if i < RING - 1:
                got = lax.ppermute(total, ALL, x_perm)
        return total

    def z_ring(parts):
        total = parts[0]
        for i in range(1, RING):
            got = lax.ppermute(total, ALL, z_perm).astype(F32)
            total = parts[i].astype(F32) + got
            if i < RING - 1:
                total = total.astype(BF16)
        return total

    grad_down = z_ring(x_ring(1, hidden, 0, FF))
    grad_gate = z_ring(x_ring(0, d_gate, 0, FF))
    back = exchange(back_pass(hidden, d_gate, d_up, gate_w, up_w, down_w))
    grad_up = jnp.concatenate(
        [z_ring(x_ring(0, d_up, i, FF // 2)) for i in range(2)], axis=1
    )
    mixed, d_tokens, d_route = combine(target, weights, back, grad_out)
    return (mixed, d_tokens, d_route.T, grad_gate[None], grad_up[None], grad_down[None])


def solution(mesh):
    by_device = P(("dp", "expert"), None)
    by_expert = P("expert", None, None)
    by_row = P("expert", "dp", None)
    return jax.shard_map(
        on_device,
        mesh=mesh,
        in_specs=(by_device,) * 4 + (by_expert,) * 3,
        out_specs=(by_device,) * 3 + (by_row,) * 3,
        check_vma=False,
    )
```

time: 288 us -> 206 us (0.72)
  waiting for transfers between devices: 127 us -> 48.6 us
  Pallas kernels: 0 us -> 46.9 us
  blocking collectives: 0 us -> 43.8 us
  local copies, waits for them, and re-layouts: 56 us -> 14.4 us
  matrix products: 32.8 us -> 0 us
  other arithmetic: 29.6 us -> 2.69 us
  starting transfers between devices: 25.7 us -> 46.8 us
  between operations: 14.3 us -> 0.9 us
    all_to_all x4 -> x1, waiting for transfers between devices: 115 us -> 0.01 us  [exchange(): lax.all_to_all(buffer, 'expert', split_axis=0, concat_axis=0, tiled=True)]
    ppermute x0 -> x24, waiting for transfers between devices: none -> 48.6 us  [the longest x12 29.7 us: x_ring(): got = lax.ppermute(total, ALL, x_perm)]
    pallas_call x0 -> x20, Pallas kernels: none -> 46.9 us  [the longest x16 31.5 us: partial_sum(): pl.pallas_call(partial_last_kernel if last else partial_kernel, grid_spec...]
    all_to_all x0 -> x1, blocking collectives: none -> 43.8 us  [exchange(): lax.all_to_all(buffer, 'expert', split_axis=0, concat_axis=0, tiled=True)]
    ppermute x0 -> x24, starting transfers between devices: none -> 41.4 us  [the longest x12 30.2 us: z_ring(): got = lax.ppermute(total, ALL, z_perm).astype(F32)]
    dot_general x9 -> x0, matrix products: 32.8 us -> none  [the longest x1 4.8 us: on_device(): d_hidden = jnp.dot(upstream, down_w, preferred_element_type=jnp.float32)]
    gather x4 -> x0, local copies, waits for them, and re-layouts: 20.9 us -> none  [the longest x1 6.19 us: on_device(): grad_out[source].astype(jnp.float32)]
    all_to_all x4 -> x1, starting transfers between devices: 25.5 us -> 5.46 us  [exchange(): lax.all_to_all(buffer, 'expert', split_axis=0, concat_axis=0, tiled=True)]
  transfers between devices with their start and end apart: 5 -> 25, of which waited for: 5 -> 12; matrix products, arithmetic and copies ran while one was open for 22% -> 1% of each run, Pallas kernels for 0% -> 15%
where the time goes in v1:
time: 206 us; the launch traced here: 204 us
  waiting for transfers between devices  48.6 us (24%)
  Pallas kernels  46.9 us (23%)
  starting transfers between devices  46.8 us (23%)
  blocking collectives  43.8 us (21%)
  local copies, waits for them, and re-layouts  14.4 us (7%)
  other arithmetic  2.69 us (1%)
    all_to_all x1, blocking collectives, exchange(): lax.all_to_all(buffer, 'expert', split_axis=0, concat_axis=0, tiled=True)  43.8 us
    pallas_call x16, Pallas kernels, partial_sum(): pl.pallas_call(partial_last_kernel if last else partial_kernel, grid_spec...  31.5 us
    ppermute x12, starting transfers between devices, z_ring(): got = lax.ppermute(total, ALL, z_perm).astype(F32)  30.2 us
    ppermute x12, waiting for transfers between devices, x_ring(): got = lax.ppermute(total, ALL, x_perm)  29.7 us
    ppermute x12, waiting for transfers between devices, z_ring(): got = lax.ppermute(total, ALL, z_perm).astype(F32)  18.8 us
    unnamed x48, local copies, waits for them, and re-layouts  14.1 us
    ppermute x12, starting transfers between devices, x_ring(): got = lax.ppermute(total, ALL, x_perm)  11.2 us
    all_to_all x1, starting transfers between devices, exchange(): lax.all_to_all(buffer, 'expert', split_axis=0, concat_axis=0, tiled=True)  5.46 us
  transfers between devices with their start and end apart: 25, of which 12 were waited for; matrix products, arithmetic and copies ran while one was open for 1% of the time, Pallas kernels for 15%

profile of v1, /device:TPU:32, one launch (start us, length us, event | category | flops | bytes accessed | tf_op | source)
XLA Modules:
  0.0 204.1 jit_solution(8167815960406594781)
XLA Ops:
  4.1 1.2 place_rows.1
  5.3 43.8 %all_to_all.10 = bf16[16,24,4096]{2,1,0:T(8,128)(2,1)S(1)} all-to-all(bf16[16,24,4096]{2,1,0:T(8,128)(2,1)S(1)} %bitcast.48), channel_id=1, replica_groups=mesh['dp'=16,'expert'=16] {'expert'}, dimensions={0} | all-to-all | bytes 6291456 | tf_op jit(solution)/shard_map/all_to_all | solution.py:245
  49.1 1.9 copy-done.15
  51.0 5.0 %hidden_pass.1 = (bf16[384,768]{1,0:T(8,128)(2,1)S(1)}, bf16[384,768]{1,0:T(8,128)(2,1)S(1)}, bf16[384,768]{1,0:T(8,128)(2,1)S(1)}) custom-call(bf16[384,4096]{1,0:T(8,128)(2,1)S(1)} %bitcast.24, bf16[2048,768]{1,0:T(8,128)(2,1)S(1)} %bitcast.42, bf16[2048,768]{1,0:T(8,128)(2,1)S(1)} %bitcast.44, bf16[2048,768]{1,0:T(8,128)(2,1)S(1)} %bitcast.46), custom_call_target="tpu_custom_call" | custom-call | flops 3623878656 | bytes 14680064 | tf_op jit(solution)/shard_map/hidden_pass/pallas_call | solution.py:106
  56.1 4.6 %back_pass.1 = bf16[384,4096]{1,0:T(8,128)(2,1)S(1)} custom-call(bf16[384,768]{1,0:T(8,128)(2,1)S(1)} %get-tuple-element.32.hidden_ref.rhs_ref, bf16[384,768]{1,0:T(8,128)(2,1)S(1)} %get-tuple-element.33.d_gate_ref.rhs_ref, bf16[384,768]{1,0:T(8,128)(2,1)S(1)} %get-tuple-element.34.d_up_ref.rhs_ref, bf16[2048,768]{1,0:T(8,128)(2,1)S(1)} %bitcast.43, ...), custom_call_target="tpu_custom_call" | custom-call | flops 3623878656 | bytes 14680064 | tf_op jit(solution)/shard_map/back_pass/pallas_call | solution.py:133
  60.8 1.7 copy-done.12
  62.5 5.5 %all-to-all-start.1 = ((bf16[16,24,4096]{2,1,0:T(8,128)(2,1)}), bf16[16,24,4096]{2,1,0:T(8,128)(2,1)}, u32[]{:S(2)}, u32[]{:S(2)}) async-start(bf16[16,24,4096]{2,1,0:T(8,128)(2,1)} %bitcast.41), calls=%async_computation.1 | async-start | bytes 6291456 | tf_op jit(solution)/shard_map/all_to_all | solution.py:245
  69.1 2.1 %partial_sum.21 = bf16[512,768]{1,0:T(8,128)(2,1)} custom-call(s32[5]{0:T(128)S(1)} %stack.59.at_ref, bf16[384,4096]{1,0:T(8,128)(2,1)S(1)} %bitcast.25, bf16[384,768]{1,0:T(8,128)(2,1)S(1)} %copy-done.9), custom_call_target="tpu_custom_call" | custom-call | flops 301989888 | bytes 3145728 | tf_op jit(solution)/shard_map/partial_sum/pallas_call | solution.py:179
  71.2 1.5 collective-permute-start.18
  72.7 1.7 partial_sum.15
  74.5 1.5 collective-permute-start.6
  75.9 1.8 partial_sum.18
  77.7 1.2 collective-permute-start.12
  79.0 9.9 %collective-permute-done.6.refs_0_ = bf16[512,384]{1,0:T(8,128)(2,1)S(1)} collective-permute-done((bf16[512,384]{1,0:T(8,128)(2,1)}, bf16[512,384]{1,0:T(8,128)(2,1)S(1)}, u32[]{:S(2)}, u32[]{:S(2)}) %collective-permute-start.6) | collective-permute-done | bytes 393248 | tf_op jit(solution)/shard_map/ppermute | solution.py:257
  93.0 2.1 %partial_sum.12 = bf16[512,768]{1,0:T(8,128)(2,1)} custom-call(s32[5]{0:T(128)S(1)} %stack.59.at_ref, bf16[384,4096]{1,0:T(8,128)(2,1)S(1)} %bitcast.29, bf16[384,768]{1,0:T(8,128)(2,1)S(1)} %copy-done.6), custom_call_target="tpu_custom_call" | custom-call | flops 301989888 | bytes 3145728 | tf_op jit(solution)/shard_map/partial_sum/pallas_call | solution.py:179
  95.1 1.5 collective-permute-start
  96.6 2.8 %partial_sum.19 = bf16[512,384]{1,0:T(8,128)(2,1)} custom-call(s32[5]{0:T(128)S(1)} %stack.57.at_ref, bf16[384,4096]{1,0:T(8,128)(2,1)S(1)} %bitcast.30, bf16[384,768]{1,0:T(8,128)(2,1)S(1)} %copy-done.2, bf16[512,384]{1,0:T(8,128)(2,1)} %collective-permute-done.12.refs_0_), custom_call_target="tpu_custom_call" | custom-call | flops 150994944 | bytes 3145728 | tf_op jit(solution)/shard_map/partial_sum/pallas_call | solution.py:179
  99.4 1.2 collective-permute-start.13
  100.6 3.3 %partial_sum.22 = bf16[512,768]{1,0:T(8,128)(2,1)} custom-call(s32[5]{0:T(128)S(1)} %stack.57.at_ref, bf16[384,4096]{1,0:T(8,128)(2,1)S(1)} %bitcast.31, bf16[384,768]{1,0:T(8,128)(2,1)S(1)} %copy-done.10, bf16[512,768]{1,0:T(8,128)(2,1)} %collective-permute-done.18.refs_0_), custom_call_target="tpu_custom_call" | custom-call | flops 301989888 | bytes 3145728 | tf_op jit(solution)/shard_map/partial_sum/pallas_call | solution.py:179
  103.9 1.7 collective-permute-start.19
  106.7 2.8 %partial_sum.17 = bf16[512,384]{1,0:T(8,128)(2,1)} custom-call(s32[5]{0:T(128)S(1)} %stack.55.at_ref, bf16[384,4096]{1,0:T(8,128)(2,1)S(1)} %bitcast.32, bf16[384,768]{1,0:T(8,128)(2,1)S(1)} %copy-done.3, bf16[512,384]{1,0:T(8,128)(2,1)} %collective-permute-done.7.refs_0_), custom_call_target="tpu_custom_call" | custom-call | flops 150994944 | bytes 3145728 | tf_op jit(solution)/shard_map/partial_sum/pallas_call | solution.py:179
  109.8 4.7 %collective-permute-done.13.refs_0_ = bf16[512,384]{1,0:T(8,128)(2,1)} collective-permute-done((bf16[512,384]{1,0:T(8,128)(2,1)}, bf16[512,384]{1,0:T(8,128)(2,1)}, u32[]{:S(2)}, u32[]{:S(2)}) %collective-permute-start.13) | collective-permute-done | bytes 393248 | tf_op jit(solution)/shard_map/ppermute | solution.py:257
  114.5 2.8 %partial_sum.20 = bf16[512,384]{1,0:T(8,128)(2,1)} custom-call(s32[5]{0:T(128)S(1)} %stack.55.at_ref, bf16[384,4096]{1,0:T(8,128)(2,1)S(1)} %bitcast.33, bf16[384,768]{1,0:T(8,128)(2,1)S(1)} %copy-done.3, bf16[512,384]{1,0:T(8,128)(2,1)} %collective-permute-done.13.refs_0_), custom_call_target="tpu_custom_call" | custom-call | flops 150994944 | bytes 3145728 | tf_op jit(solution)/shard_map/partial_sum/pallas_call | solution.py:179
  117.3 9.8 %collective-permute-done.8.got_ref = bf16[512,384]{1,0:T(8,128)(2,1)} collective-permute-done((bf16[512,384]{1,0:T(8,128)(2,1)}, bf16[512,384]{1,0:T(8,128)(2,1)}, u32[]{:S(2)}, u32[]{:S(2)}) %collective-permute-start.8) | collective-permute-done | bytes 393248 | tf_op jit(solution)/shard_map/ppermute | solution.py:257
  128.2 2.1 %partial_last.5 = (bf16[128,384]{1,0:T(8,128)(2,1)S(1)}, bf16[128,384]{1,0:T(8,128)(2,1)S(1)}, bf16[128,384]{1,0:T(8,128)(2,1)S(1)}, bf16[128,384]{1,0:T(8,128)(2,1)S(1)}) custom-call(s32[5]{0:T(128)S(1)} %stack.53.at_ref, bf16[384,4096]{1,0:T(8,128)(2,1)S(1)} %bitcast.34, bf16[384,768]{1,0:T(8,128)(2,1)S(1)} %copy-done.4, ...), custom_call_target="tpu_custom_call" | custom-call | flops 150994944 | bytes 3145728 | tf_op jit(solution)/shard_map/partial_last/pallas_call | solution.py:179
  130.2 3.3 %collective-permute-start.9 = (bf16[128,384]{1,0:T(8,128)(2,1)S(1)}, bf16[128,384]{1,0:T(8,128)(2,1)S(1)}, u32[]{:S(2)}, u32[]{:S(2)}) collective-permute-start(bf16[128,384]{1,0:T(8,128)(2,1)S(1)} %get-tuple-element.45), channel_id=1, source_target_pairs={{0,16},{1,49},{2,18},{3,51},{4,20},{5,53},{6,22},{7,55},{8,24},{9,... | collective-permute-start | bytes 294920 | tf_op jit(solution)/shard_map/ppermute | solution.py:263
  133.6 2.3 %partial_sum.13 = bf16[512,768]{1,0:T(8,128)(2,1)S(1)} custom-call(s32[5]{0:T(128)S(1)} %stack.57.at_ref, bf16[384,4096]{1,0:T(8,128)(2,1)S(1)} %bitcast.35, bf16[384,768]{1,0:T(8,128)(2,1)S(1)} %copy-done.7, bf16[512,768]{1,0:T(8,128)(2,1)} %collective-permute-done.refs_0_), custom_call_target="tpu_custom_call" | custom-call | flops 301989888 | bytes 3145728 | tf_op jit(solution)/shard_map/partial_sum/pallas_call | solution.py:179
  137.0 3.6 %collective-permute-start.15 = (bf16[128,384]{1,0:T(8,128)(2,1)S(1)}, bf16[128,384]{1,0:T(8,128)(2,1)S(1)}, u32[]{:S(2)}, u32[]{:S(2)}) collective-permute-start(bf16[128,384]{1,0:T(8,128)(2,1)S(1)} %get-tuple-element.49), channel_id=1, source_target_pairs={{0,16},{1,49},{2,18},{3,51},{4,20},{5,53},{6,22},{7,55},{8,24},{9,... | collective-permute-start | bytes 294920 | tf_op jit(solution)/shard_map/ppermute | solution.py:263
  140.7 1.6 collective-permute-start.10
  142.3 2.3 %partial_sum.23 = bf16[512,768]{1,0:T(8,128)(2,1)S(1)} custom-call(s32[5]{0:T(128)S(1)} %stack.55.at_ref, bf16[384,4096]{1,0:T(8,128)(2,1)S(1)} %bitcast.37, bf16[384,768]{1,0:T(8,128)(2,1)S(1)} %copy-done.11, bf16[512,768]{1,0:T(8,128)(2,1)} %collective-permute-done.19.refs_0_), custom_call_target="tpu_custom_call" | custom-call | flops 301989888 | bytes 3145728 | tf_op jit(solution)/shard_map/partial_sum/pallas_call | solution.py:179
  145.2 2.4 %collective-permute-start.16 = (bf16[128,384]{1,0:T(8,128)(2,1)S(1)}, bf16[128,384]{1,0:T(8,128)(2,1)S(1)}, u32[]{:S(2)}, u32[]{:S(2)}) collective-permute-start(bf16[128,384]{1,0:T(8,128)(2,1)S(1)} %add_convert_fusion.5), channel_id=1, source_target_pairs={{0,16},{1,49},{2,18},{3,51},{4,20},{5,53},{6,22},{7,55},{8,24},{9,... | collective-permute-start | bytes 294920 | tf_op jit(solution)/shard_map/ppermute | solution.py:263
  148.4 1.5 collective-permute-start.11
  151.2 1.3 collective-permute-start.2
  153.0 2.1 %collective-permute-start.17 = (bf16[128,384]{1,0:T(8,128)(2,1)S(1)}, bf16[128,384]{1,0:T(8,128)(2,1)S(1)}, u32[]{:S(2)}, u32[]{:S(2)}) collective-permute-start(bf16[128,384]{1,0:T(8,128)(2,1)S(1)} %add_convert_fusion.4), channel_id=1, source_target_pairs={{0,16},{1,49},{2,18},{3,51},{4,20},{5,53},{6,22},{7,55},{8,24},{9,... | collective-permute-start | bytes 294920 | tf_op jit(solution)/shard_map/ppermute | solution.py:263
  155.5 2.3 %collective-permute-done.20.got_ref = bf16[512,768]{1,0:T(8,128)(2,1)S(1)} collective-permute-done((bf16[512,768]{1,0:T(8,128)(2,1)S(1)}, bf16[512,768]{1,0:T(8,128)(2,1)S(1)}, u32[]{:S(2)}, u32[]{:S(2)}) %collective-permute-start.20) | collective-permute-done | bytes 786464 | tf_op jit(solution)/shard_map/ppermute | solution.py:257
  157.8 1.2 partial_last.7
  159.0 3.4 %collective-permute-start.21 = (bf16[128,768]{1,0:T(8,128)(2,1)S(1)}, bf16[128,768]{1,0:T(8,128)(2,1)S(1)}, u32[]{:S(2)}, u32[]{:S(2)}) collective-permute-start(bf16[128,768]{1,0:T(8,128)(2,1)S(1)} %get-tuple-element.53), channel_id=1, source_target_pairs={{0,16},{1,49},{2,18},{3,51},{4,20},{5,53},{6,22},{7,55},{8,24},{9,... | collective-permute-start | bytes 589832 | tf_op jit(solution)/shard_map/ppermute | solution.py:263
  163.2 3.1 %collective-permute-done.2.got_ref = bf16[512,768]{1,0:T(8,128)(2,1)S(1)} collective-permute-done((bf16[512,768]{1,0:T(8,128)(2,1)S(1)}, bf16[512,768]{1,0:T(8,128)(2,1)S(1)}, u32[]{:S(2)}, u32[]{:S(2)}) %collective-permute-start.2) | collective-permute-done | bytes 786464 | tf_op jit(solution)/shard_map/ppermute | solution.py:257
  167.5 3.4 %collective-permute-start.3 = (bf16[128,768]{1,0:T(8,128)(2,1)S(1)}, bf16[128,768]{1,0:T(8,128)(2,1)S(1)}, u32[]{:S(2)}, u32[]{:S(2)}) collective-permute-start(bf16[128,768]{1,0:T(8,128)(2,1)S(1)} %get-tuple-element.41), channel_id=1, source_target_pairs={{0,16},{1,49},{2,18},{3,51},{4,20},{5,53},{6,22},{7,55},{8,24},{9,... | collective-permute-start | bytes 589832 | tf_op jit(solution)/shard_map/ppermute | solution.py:263
  170.9 1.6 collective-permute-start.22
  172.5 6.7 %collective-permute-done.3 = bf16[128,768]{1,0:T(8,128)(2,1)S(1)} collective-permute-done((bf16[128,768]{1,0:T(8,128)(2,1)S(1)}, bf16[128,768]{1,0:T(8,128)(2,1)S(1)}, u32[]{:S(2)}, u32[]{:S(2)}) %collective-permute-start.3) | collective-permute-done | bytes 196640 | tf_op jit(solution)/shard_map/ppermute | solution.py:263
  179.2 2.4 %collective-permute-start.4 = (bf16[128,768]{1,0:T(8,128)(2,1)S(1)}, bf16[128,768]{1,0:T(8,128)(2,1)S(1)}, u32[]{:S(2)}, u32[]{:S(2)}) collective-permute-start(bf16[128,768]{1,0:T(8,128)(2,1)S(1)} %add_convert_fusion.3), channel_id=1, source_target_pairs={{0,16},{1,49},{2,18},{3,51},{4,20},{5,53},{6,22},{7,55},{8,24},{9,... | collective-permute-start | bytes 589832 | tf_op jit(solution)/shard_map/ppermute | solution.py:263
  181.6 2.9 %collective-permute-start.23 = (bf16[128,768]{1,0:T(8,128)(2,1)S(1)}, bf16[128,768]{1,0:T(8,128)(2,1)S(1)}, u32[]{:S(2)}, u32[]{:S(2)}) collective-permute-start(bf16[128,768]{1,0:T(8,128)(2,1)S(1)} %add_convert_fusion), channel_id=1, source_target_pairs={{0,16},{1,49},{2,18},{3,51},{4,20},{5,53},{6,22},{7,55},{8,24},{9,... | collective-permute-start | bytes 589832 | tf_op jit(solution)/shard_map/ppermute | solution.py:263
  184.5 2.6 %collective-permute-done.4 = bf16[128,768]{1,0:T(8,128)(2,1)S(1)} collective-permute-done((bf16[128,768]{1,0:T(8,128)(2,1)S(1)}, bf16[128,768]{1,0:T(8,128)(2,1)S(1)}, u32[]{:S(2)}, u32[]{:S(2)}) %collective-permute-start.4) | collective-permute-done | bytes 196640 | tf_op jit(solution)/shard_map/ppermute | solution.py:263
  187.2 1.9 collective-permute-start.5
  189.1 1.3 collective-permute-done.23
  191.2 6.6 %collective-permute-done.5 = bf16[128,768]{1,0:T(8,128)(2,1)S(1)} collective-permute-done((bf16[128,768]{1,0:T(8,128)(2,1)S(1)}, bf16[128,768]{1,0:T(8,128)(2,1)S(1)}, u32[]{:S(2)}, u32[]{:S(2)}) %collective-permute-start.5) | collective-permute-done | bytes 196640 | tf_op jit(solution)/shard_map/ppermute | solution.py:263
  199.7 4.4 %combine_rows.1 = (bf16[128,2048]{1,0:T(8,128)(2,1)}, bf16[128,2048]{1,0:T(8,128)(2,1)}, f32[6,128]{1,0:T(8,128)}) custom-call(s32[6,128]{1,0:T(8,128)S(1)} %get-tuple-element.30.target_ref, f32[6,128]{1,0:T(8,128)S(1)} %bitcast.51, bf16[384,4096]{1,0:T(8,128)(2,1)} %bitcast.8.back_ref, bf16[128,2048]{1,0:T(8,128)(2,1)S(1)} %copy-done.20), custom_call_target="tpu_custom_call" | custom-call | flops 1000000000 | bytes 6291456 | tf_op jit(solution)/shard_map/combine_rows/pallas_call | solution.py:220
  (88 shorter events, 21.0 us)
Async XLA Ops:
  0.6 1.0 copy-start.18
  1.7 1.0 copy-start.19
  2.7 0.7 copy-start.21
  5.3 43.9 %copy-start.13 = (bf16[1,2048,768]{2,1,0:T(8,128)(2,1)S(1)}, bf16[1,2048,768]{2,1,0:T(8,128)(2,1)}, u32[]{:S(2)}) copy-start(bf16[1,2048,768]{2,1,0:T(8,128)(2,1)} %param.11) | copy-start | bytes 9437188
  5.3 43.8 %copy-start.14 = (bf16[1,2048,768]{2,1,0:T(8,128)(2,1)S(1)}, bf16[1,2048,768]{2,1,0:T(8,128)(2,1)}, u32[]{:S(2)}) copy-start(bf16[1,2048,768]{2,1,0:T(8,128)(2,1)} %param.12) | copy-start | bytes 9437188
  49.1 1.9 copy-start.15
  56.1 4.7 %copy-start = (bf16[384,768]{1,0:T(8,128)(2,1)}, bf16[384,768]{1,0:T(8,128)(2,1)S(1)}, u32[]{:S(2)}) copy-start(bf16[384,768]{1,0:T(8,128)(2,1)S(1)} %get-tuple-element.34.d_up_ref.rhs_ref) | copy-start | bytes 1769476
  56.1 4.7 %copy-start.5 = (bf16[384,768]{1,0:T(8,128)(2,1)}, bf16[384,768]{1,0:T(8,128)(2,1)S(1)}, u32[]{:S(2)}) copy-start(bf16[384,768]{1,0:T(8,128)(2,1)S(1)} %get-tuple-element.33.d_gate_ref.rhs_ref) | copy-start | bytes 1769476
  56.1 4.7 %copy-start.8 = (bf16[384,768]{1,0:T(8,128)(2,1)}, bf16[384,768]{1,0:T(8,128)(2,1)S(1)}, u32[]{:S(2)}) copy-start(bf16[384,768]{1,0:T(8,128)(2,1)S(1)} %get-tuple-element.32.hidden_ref.rhs_ref) | copy-start | bytes 1769476
  60.8 1.7 copy-start.12
  62.5 136.2 %all-to-all-start.1 = ((bf16[16,24,4096]{2,1,0:T(8,128)(2,1)}), bf16[16,24,4096]{2,1,0:T(8,128)(2,1)}, u32[]{:S(2)}, u32[]{:S(2)}) async-start(bf16[16,24,4096]{2,1,0:T(8,128)(2,1)} %bitcast.41), calls=%async_computation.1 | async-start | bytes 6291456 | tf_op jit(solution)/shard_map/all_to_all | solution.py:245
  68.0 1.1 copy-start.9
  69.1 3.6 %copy-start.1 = (bf16[384,768]{1,0:T(8,128)(2,1)S(1)}, bf16[384,768]{1,0:T(8,128)(2,1)}, u32[]{:S(2)}) copy-start(bf16[384,768]{1,0:T(8,128)(2,1)} %copy-done) | copy-start | bytes 1769476
  71.2 29.4 %collective-permute-start.18 = (bf16[512,768]{1,0:T(8,128)(2,1)}, bf16[512,768]{1,0:T(8,128)(2,1)}, u32[]{:S(2)}, u32[]{:S(2)}) collective-permute-start(bf16[512,768]{1,0:T(8,128)(2,1)} %partial_sum.21), channel_id=1, source_target_pairs={{0,64},{1,193},{2,66},{3,195},{4,68},{5,197},{6,70},{7,199},{8,72}... | collective-permute-start | bytes 2359304 | tf_op jit(solution)/shard_map/ppermute | solution.py:257
  74.5 14.4 %collective-permute-start.6 = (bf16[512,384]{1,0:T(8,128)(2,1)}, bf16[512,384]{1,0:T(8,128)(2,1)S(1)}, u32[]{:S(2)}, u32[]{:S(2)}) collective-permute-start(bf16[512,384]{1,0:T(8,128)(2,1)} %partial_sum.15), channel_id=1, source_target_pairs={{0,64},{1,193},{2,66},{3,195},{4,68},{5,197},{6,70},{7,199},{8,72}... | collective-permute-start | bytes 1179656 | tf_op jit(solution)/shard_map/ppermute | solution.py:257
  77.7 18.9 %collective-permute-start.12 = (bf16[512,384]{1,0:T(8,128)(2,1)}, bf16[512,384]{1,0:T(8,128)(2,1)}, u32[]{:S(2)}, u32[]{:S(2)}) collective-permute-start(bf16[512,384]{1,0:T(8,128)(2,1)} %partial_sum.18), channel_id=1, source_target_pairs={{0,64},{1,193},{2,66},{3,195},{4,68},{5,197},{6,70},{7,199},{8,72}... | collective-permute-start | bytes 1179656 | tf_op jit(solution)/shard_map/ppermute | solution.py:257
  88.8 0.7 copy-start.16
  89.6 1.1 copy-start.2
  90.7 1.0 copy-start.17
  91.6 1.4 copy-start.6
  92.6 13.0 %collective-permute-start.7 = (bf16[512,384]{1,0:T(8,128)(2,1)S(1)}, bf16[512,384]{1,0:T(8,128)(2,1)}, u32[]{:S(2)}, u32[]{:S(2)}) collective-permute-start(bf16[512,384]{1,0:T(8,128)(2,1)S(1)} %partial_sum.16), channel_id=1, source_target_pairs={{0,64},{1,193},{2,66},{3,195},{4,68},{5,197},{6,70},{7,199},{8,72}... | collective-permute-start | bytes 1179656 | tf_op jit(solution)/shard_map/ppermute | solution.py:257
  95.1 5.5 %copy-start.10 = (bf16[384,768]{1,0:T(8,128)(2,1)S(1)}, bf16[384,768]{1,0:T(8,128)(2,1)}, u32[]{:S(2)}) copy-start(bf16[384,768]{1,0:T(8,128)(2,1)} %copy-done.8) | copy-start | bytes 1769476
  95.1 38.4 %collective-permute-start = (bf16[512,768]{1,0:T(8,128)(2,1)}, bf16[512,768]{1,0:T(8,128)(2,1)}, u32[]{:S(2)}, u32[]{:S(2)}) collective-permute-start(bf16[512,768]{1,0:T(8,128)(2,1)} %partial_sum.12), channel_id=1, source_target_pairs={{0,64},{1,193},{2,66},{3,195},{4,68},{5,197},{6,70},{7,199},{8,72}... | collective-permute-start | bytes 2359304 | tf_op jit(solution)/shard_map/ppermute | solution.py:257
  99.4 15.0 %collective-permute-start.13 = (bf16[512,384]{1,0:T(8,128)(2,1)}, bf16[512,384]{1,0:T(8,128)(2,1)}, u32[]{:S(2)}, u32[]{:S(2)}) collective-permute-start(bf16[512,384]{1,0:T(8,128)(2,1)} %partial_sum.19), channel_id=1, source_target_pairs={{0,64},{1,193},{2,66},{3,195},{4,68},{5,197},{6,70},{7,199},{8,72}... | collective-permute-start | bytes 1179656 | tf_op jit(solution)/shard_map/ppermute | solution.py:257
  103.9 38.4 %collective-permute-start.19 = (bf16[512,768]{1,0:T(8,128)(2,1)}, bf16[512,768]{1,0:T(8,128)(2,1)}, u32[]{:S(2)}, u32[]{:S(2)}) collective-permute-start(bf16[512,768]{1,0:T(8,128)(2,1)} %partial_sum.22), channel_id=1, source_target_pairs={{0,64},{1,193},{2,66},{3,195},{4,68},{5,197},{6,70},{7,199},{8,72}... | collective-permute-start | bytes 2359304 | tf_op jit(solution)/shard_map/ppermute | solution.py:257
  105.7 1.1 copy-start.3
  109.5 17.6 %collective-permute-start.8 = (bf16[512,384]{1,0:T(8,128)(2,1)}, bf16[512,384]{1,0:T(8,128)(2,1)}, u32[]{:S(2)}, u32[]{:S(2)}) collective-permute-start(bf16[512,384]{1,0:T(8,128)(2,1)} %partial_sum.17), channel_id=1, source_target_pairs={{0,64},{1,193},{2,66},{3,195},{4,68},{5,197},{6,70},{7,199},{8,72}... | collective-permute-start | bytes 1179656 | tf_op jit(solution)/shard_map/ppermute | solution.py:257
  117.2 18.7 %collective-permute-start.14 = (bf16[512,384]{1,0:T(8,128)(2,1)}, bf16[512,384]{1,0:T(8,128)(2,1)S(1)}, u32[]{:S(2)}, u32[]{:S(2)}) collective-permute-start(bf16[512,384]{1,0:T(8,128)(2,1)} %partial_sum.20), channel_id=1, source_target_pairs={{0,64},{1,193},{2,66},{3,195},{4,68},{5,197},{6,70},{7,199},{8,72}... | collective-permute-start | bytes 1179656 | tf_op jit(solution)/shard_map/ppermute | solution.py:257
  127.1 1.1 copy-start.4
  128.2 5.4 %copy-start.7 = (bf16[384,768]{1,0:T(8,128)(2,1)S(1)}, bf16[384,768]{1,0:T(8,128)(2,1)}, u32[]{:S(2)}) copy-start(bf16[384,768]{1,0:T(8,128)(2,1)} %copy-done.5) | copy-start | bytes 1769476
  130.2 10.5 %collective-permute-start.9 = (bf16[128,384]{1,0:T(8,128)(2,1)S(1)}, bf16[128,384]{1,0:T(8,128)(2,1)S(1)}, u32[]{:S(2)}, u32[]{:S(2)}) collective-permute-start(bf16[128,384]{1,0:T(8,128)(2,1)S(1)} %get-tuple-element.45), channel_id=1, source_target_pairs={{0,16},{1,49},{2,18},{3,51},{4,20},{5,53},{6,22},{7,55},{8,24},{9,... | collective-permute-start | bytes 294920 | tf_op jit(solution)/shard_map/ppermute | solution.py:263
  135.9 6.4 %copy-start.11 = (bf16[384,768]{1,0:T(8,128)(2,1)S(1)}, bf16[384,768]{1,0:T(8,128)(2,1)}, u32[]{:S(2)}) copy-start(bf16[384,768]{1,0:T(8,128)(2,1)} %copy-done.8) | copy-start | bytes 1769476
  135.9 14.1 %collective-permute-start.1 = (bf16[512,768]{1,0:T(8,128)(2,1)S(1)}, bf16[512,768]{1,0:T(8,128)(2,1)S(1)}, u32[]{:S(2)}, u32[]{:S(2)}) collective-permute-start(bf16[512,768]{1,0:T(8,128)(2,1)S(1)} %partial_sum.13), channel_id=1, source_target_pairs={{0,64},{1,193},{2,66},{3,195},{4,68},{5,197},{6,70},{7,199},{8,72}... | collective-permute-start | bytes 2359304 | tf_op jit(solution)/shard_map/ppermute | solution.py:257
  137.0 8.2 %collective-permute-start.15 = (bf16[128,384]{1,0:T(8,128)(2,1)S(1)}, bf16[128,384]{1,0:T(8,128)(2,1)S(1)}, u32[]{:S(2)}, u32[]{:S(2)}) collective-permute-start(bf16[128,384]{1,0:T(8,128)(2,1)S(1)} %get-tuple-element.49), channel_id=1, source_target_pairs={{0,16},{1,49},{2,18},{3,51},{4,20},{5,53},{6,22},{7,55},{8,24},{9,... | collective-permute-start | bytes 294920 | tf_op jit(solution)/shard_map/ppermute | solution.py:263
  140.7 7.7 %collective-permute-start.10 = (bf16[128,384]{1,0:T(8,128)(2,1)S(1)}, bf16[128,384]{1,0:T(8,128)(2,1)S(1)}, u32[]{:S(2)}, u32[]{:S(2)}) collective-permute-start(bf16[128,384]{1,0:T(8,128)(2,1)S(1)} %add_convert_fusion.7), channel_id=1, source_target_pairs={{0,16},{1,49},{2,18},{3,51},{4,20},{5,53},{6,22},{7,55},{8,24},{9,... | collective-permute-start | bytes 294920 | tf_op jit(solution)/shard_map/ppermute | solution.py:263
  144.6 13.3 %collective-permute-start.20 = (bf16[512,768]{1,0:T(8,128)(2,1)S(1)}, bf16[512,768]{1,0:T(8,128)(2,1)S(1)}, u32[]{:S(2)}, u32[]{:S(2)}) collective-permute-start(bf16[512,768]{1,0:T(8,128)(2,1)S(1)} %partial_sum.23), channel_id=1, source_target_pairs={{0,64},{1,193},{2,66},{3,195},{4,68},{5,197},{6,70},{7,199},{8,72}... | collective-permute-start | bytes 2359304 | tf_op jit(solution)/shard_map/ppermute | solution.py:257
  145.2 7.8 %collective-permute-start.16 = (bf16[128,384]{1,0:T(8,128)(2,1)S(1)}, bf16[128,384]{1,0:T(8,128)(2,1)S(1)}, u32[]{:S(2)}, u32[]{:S(2)}) collective-permute-start(bf16[128,384]{1,0:T(8,128)(2,1)S(1)} %add_convert_fusion.5), channel_id=1, source_target_pairs={{0,16},{1,49},{2,18},{3,51},{4,20},{5,53},{6,22},{7,55},{8,24},{9,... | collective-permute-start | bytes 294920 | tf_op jit(solution)/shard_map/ppermute | solution.py:263
  148.4 7.0 %collective-permute-start.11 = (bf16[128,384]{1,0:T(8,128)(2,1)S(1)}, bf16[128,384]{1,0:T(8,128)(2,1)S(1)}, u32[]{:S(2)}, u32[]{:S(2)}) collective-permute-start(bf16[128,384]{1,0:T(8,128)(2,1)S(1)} %add_convert_fusion.6), channel_id=1, source_target_pairs={{0,16},{1,49},{2,18},{3,51},{4,20},{5,53},{6,22},{7,55},{8,24},{9,... | collective-permute-start | bytes 294920 | tf_op jit(solution)/shard_map/ppermute | solution.py:263
  151.2 15.1 %collective-permute-start.2 = (bf16[512,768]{1,0:T(8,128)(2,1)S(1)}, bf16[512,768]{1,0:T(8,128)(2,1)S(1)}, u32[]{:S(2)}, u32[]{:S(2)}) collective-permute-start(bf16[512,768]{1,0:T(8,128)(2,1)S(1)} %partial_sum.14), channel_id=1, source_target_pairs={{0,64},{1,193},{2,66},{3,195},{4,68},{5,197},{6,70},{7,199},{8,72}... | collective-permute-start | bytes 2359304 | tf_op jit(solution)/shard_map/ppermute | solution.py:257
  153.0 9.4 %collective-permute-start.17 = (bf16[128,384]{1,0:T(8,128)(2,1)S(1)}, bf16[128,384]{1,0:T(8,128)(2,1)S(1)}, u32[]{:S(2)}, u32[]{:S(2)}) collective-permute-start(bf16[128,384]{1,0:T(8,128)(2,1)S(1)} %add_convert_fusion.4), channel_id=1, source_target_pairs={{0,16},{1,49},{2,18},{3,51},{4,20},{5,53},{6,22},{7,55},{8,24},{9,... | collective-permute-start | bytes 294920 | tf_op jit(solution)/shard_map/ppermute | solution.py:263
  159.0 11.8 %collective-permute-start.21 = (bf16[128,768]{1,0:T(8,128)(2,1)S(1)}, bf16[128,768]{1,0:T(8,128)(2,1)S(1)}, u32[]{:S(2)}, u32[]{:S(2)}) collective-permute-start(bf16[128,768]{1,0:T(8,128)(2,1)S(1)} %get-tuple-element.53), channel_id=1, source_target_pairs={{0,16},{1,49},{2,18},{3,51},{4,20},{5,53},{6,22},{7,55},{8,24},{9,... | collective-permute-start | bytes 589832 | tf_op jit(solution)/shard_map/ppermute | solution.py:263
  163.2 35.4 %copy-start.23 = (f32[128,6]{0,1:T(8,128)S(1)}, f32[128,6]{0,1:T(8,128)}, u32[]{:S(2)}) copy-start(f32[128,6]{0,1:T(8,128)} %param.10) | copy-start | bytes 9220
  167.5 11.7 %collective-permute-start.3 = (bf16[128,768]{1,0:T(8,128)(2,1)S(1)}, bf16[128,768]{1,0:T(8,128)(2,1)S(1)}, u32[]{:S(2)}, u32[]{:S(2)}) collective-permute-start(bf16[128,768]{1,0:T(8,128)(2,1)S(1)} %get-tuple-element.41), channel_id=1, source_target_pairs={{0,16},{1,49},{2,18},{3,51},{4,20},{5,53},{6,22},{7,55},{8,24},{9,... | collective-permute-start | bytes 589832 | tf_op jit(solution)/shard_map/ppermute | solution.py:263
  170.9 10.7 %collective-permute-start.22 = (bf16[128,768]{1,0:T(8,128)(2,1)S(1)}, bf16[128,768]{1,0:T(8,128)(2,1)S(1)}, u32[]{:S(2)}, u32[]{:S(2)}) collective-permute-start(bf16[128,768]{1,0:T(8,128)(2,1)S(1)} %add_convert_fusion.1), channel_id=1, source_target_pairs={{0,16},{1,49},{2,18},{3,51},{4,20},{5,53},{6,22},{7,55},{8,24},{9,... | collective-permute-start | bytes 589832 | tf_op jit(solution)/shard_map/ppermute | solution.py:263
  179.2 8.0 %collective-permute-start.4 = (bf16[128,768]{1,0:T(8,128)(2,1)S(1)}, bf16[128,768]{1,0:T(8,128)(2,1)S(1)}, u32[]{:S(2)}, u32[]{:S(2)}) collective-permute-start(bf16[128,768]{1,0:T(8,128)(2,1)S(1)} %add_convert_fusion.3), channel_id=1, source_target_pairs={{0,16},{1,49},{2,18},{3,51},{4,20},{5,53},{6,22},{7,55},{8,24},{9,... | collective-permute-start | bytes 589832 | tf_op jit(solution)/shard_map/ppermute | solution.py:263
  181.6 8.8 %collective-permute-start.23 = (bf16[128,768]{1,0:T(8,128)(2,1)S(1)}, bf16[128,768]{1,0:T(8,128)(2,1)S(1)}, u32[]{:S(2)}, u32[]{:S(2)}) collective-permute-start(bf16[128,768]{1,0:T(8,128)(2,1)S(1)} %add_convert_fusion), channel_id=1, source_target_pairs={{0,16},{1,49},{2,18},{3,51},{4,20},{5,53},{6,22},{7,55},{8,24},{9,... | collective-permute-start | bytes 589832 | tf_op jit(solution)/shard_map/ppermute | solution.py:263
  187.2 10.6 %collective-permute-start.5 = (bf16[128,768]{1,0:T(8,128)(2,1)S(1)}, bf16[128,768]{1,0:T(8,128)(2,1)S(1)}, u32[]{:S(2)}, u32[]{:S(2)}) collective-permute-start(bf16[128,768]{1,0:T(8,128)(2,1)S(1)} %add_convert_fusion.2), channel_id=1, source_target_pairs={{0,16},{1,49},{2,18},{3,51},{4,20},{5,53},{6,22},{7,55},{8,24},{9,... | collective-permute-start | bytes 589832 | tf_op jit(solution)/shard_map/ppermute | solution.py:263
  198.6 1.0 copy-start.20
  (1 other events, 0.7 us)

commit v2 on v1

v2 whole, which is shorter than its diff:
```python
import jax
import jax.numpy as jnp
from jax import lax
from jax.experimental import pallas as pl
from jax.experimental.pallas import tpu as pltpu
from jax.sharding import PartitionSpec as P

CAP = 24
EXPERTS = 16
SLOTS = EXPERTS * CAP
ROWS = 128
TOP = 6
D = 2048
FF = 768
RING = 4
MIB = 1024 * 1024
LONG = pl.CostEstimate(flops=10**10, bytes_accessed=MIB, transcendentals=0)
STEP = pl.CostEstimate(flops=10**10, bytes_accessed=1, transcendentals=0)
SMALL = pl.CostEstimate(flops=1, bytes_accessed=1, transcendentals=0)
F32 = jnp.float32
BF16 = jnp.bfloat16
ALL = ("dp", "expert")
ORDER = (
    "first gate",
    "run back",
    "all up",
    "rest gate",
    "second gate",
    "all down",
    "third gate",
    "second up",
    "fourth gate",
    "third up",
    "second down",
    "run combine",
    "fifth gate",
    "fourth up",
    "third down",
    "fifth up",
    "fourth down",
    "fifth down",
)


def partners(core, at):
    beside, across = at ^ 1, RING - 1 - at
    first, second = (beside, across) if core == 0 else (across, beside)
    return first, second, (at + 2) % RING


def pairs_of(axis, stage):
    pairs = []
    for dp in range(RING * RING):
        x, z = divmod(dp, RING)
        for expert in range(EXPERTS):
            if axis == "x":
                to = partners(expert % 2, x)[stage] * RING + z
            else:
                to = x * RING + partners(expert % 2, z)[stage]
            pairs.append((dp * EXPERTS + expert, to * EXPERTS + expert))
    return pairs


def dot(a, b, contract):
    return lax.dot_general(a, b, ((contract[:1], contract[1:]), ((), ())), preferred_element_type=F32)


def place_kernel(at_ref, ids_ref, weights_ref, tokens_ref, grads_ref, send_ref, target_ref):
    ids = ids_ref[...]
    weights = weights_ref[...]
    expert = lax.broadcasted_iota(jnp.int32, (EXPERTS, ROWS), 0)
    picked = jnp.zeros((EXPERTS, ROWS), F32)
    for k in range(TOP):
        picked = picked + jnp.where(ids[k : k + 1, :] == expert, 1.0, 0.0)
    earlier = lax.broadcasted_iota(jnp.int32, (ROWS, ROWS), 0) < lax.broadcasted_iota(
        jnp.int32, (ROWS, ROWS), 1
    )
    position = jnp.dot(
        picked.astype(BF16),
        jnp.where(earlier, 1.0, 0.0).astype(BF16),
        preferred_element_type=F32,
    )
    slot = lax.broadcasted_iota(jnp.int32, (SLOTS, ROWS), 0)
    chosen = jnp.zeros((SLOTS, ROWS), F32)
    scale = jnp.zeros((SLOTS, ROWS), F32)
    for k in range(TOP):
        pick = ids[k : k + 1, :]
        own = jnp.sum(jnp.where(pick == expert, position, 0.0), axis=0, keepdims=True)
        place = own.astype(jnp.int32)
        target = jnp.where((pick < EXPERTS) & (place < CAP), pick * CAP + place, -1)
        target_ref[k : k + 1, :] = target
        here = target == slot
        chosen = chosen + jnp.where(here, 1.0, 0.0)
        scale = scale + jnp.where(here, weights[k : k + 1, :], 0.0)
    chosen = chosen.astype(BF16)
    slot_scale = jnp.sum(scale, axis=1, keepdims=True)
    send_ref[:, :D] = jnp.dot(chosen, tokens_ref[...], preferred_element_type=F32).astype(BF16)
    send_ref[:, D:] = (
        slot_scale * jnp.dot(chosen, grads_ref[...], preferred_element_type=F32)
    ).astype(BF16)


def place(at, ids, weights, tokens, grads):
    whole = pl.BlockSpec(memory_space=pltpu.VMEM)
    return pl.pallas_call(
        place_kernel,
        in_specs=[pl.BlockSpec(memory_space=pltpu.SMEM)] + [whole] * 4,
        out_shape=(
            jax.ShapeDtypeStruct((SLOTS, 2 * D), BF16),
            jax.ShapeDtypeStruct((TOP, ROWS), jnp.int32),
        ),
        compiler_params=pltpu.CompilerParams(vmem_limit_bytes=20 * MIB),
        cost_estimate=pl.CostEstimate(flops=4 * 10**10, bytes_accessed=5 * MIB, transcendentals=0),
        name="place_rows",
    )(at, ids, weights, tokens, grads)


def hidden_kernel(rows_ref, gate_ref, up_ref, down_ref, hidden_ref, d_gate_ref, d_up_ref):
    inputs = rows_ref[:, :D]
    gate_pre = jnp.dot(inputs, gate_ref[...], preferred_element_type=F32)
    up_pre = jnp.dot(inputs, up_ref[...], preferred_element_type=F32)
    d_hidden = jnp.dot(rows_ref[:, D:], down_ref[...], preferred_element_type=F32)
    sigmoid = jax.nn.sigmoid(gate_pre)
    silu = gate_pre * sigmoid
    hidden_ref[...] = (silu * up_pre).astype(BF16)
    d_up_ref[...] = (d_hidden * silu).astype(BF16)
    d_gate_ref[...] = (d_hidden * up_pre * sigmoid * (1.0 + gate_pre * (1.0 - sigmoid))).astype(BF16)


def hidden_pass(rows, gate_w, up_w, down_w):
    tile = 256
    weight = pl.BlockSpec((D, tile), lambda i: (0, i))
    out = pl.BlockSpec((SLOTS, tile), lambda i: (0, i))
    return pl.pallas_call(
        hidden_kernel,
        grid=(FF // tile,),
        in_specs=[pl.BlockSpec((SLOTS, 2 * D), lambda i: (0, 0)), weight, weight, weight],
        out_specs=[out] * 3,
        out_shape=[jax.ShapeDtypeStruct((SLOTS, FF), BF16)] * 3,
        compiler_params=pltpu.CompilerParams(vmem_limit_bytes=20 * MIB),
        cost_estimate=SMALL,
        name="hidden_pass",
    )(rows, gate_w, up_w, down_w)


OUT_TILE = 512
CHUNK = D // RING
ANY = pl.BlockSpec(memory_space=pl.ANY)
TOKEN = jax.ShapeDtypeStruct((8, 128), jnp.int32)


def at_zero(*shape):
    return pl.BlockSpec(shape, lambda *_: (0,) * len(shape))


def emit(token_ref):
    token_ref[...] = jnp.zeros(token_ref.shape, token_ref.dtype)


def back_kernel(
    hidden_ref, d_gate_ref, d_up_ref, gate_ref, up_ref, down_ref, after_ref, out_ref, token_ref
):
    out_ref[:, :OUT_TILE] = dot(hidden_ref[...], down_ref[...], (1, 1)).astype(BF16)
    out_ref[:, OUT_TILE:] = (
        dot(d_gate_ref[...], gate_ref[...], (1, 1)) + dot(d_up_ref[...], up_ref[...], (1, 1))
    ).astype(BF16)
    emit(token_ref)


def back_pass(hidden, d_gate, d_up, gate_w, up_w, down_w, after):
    act = at_zero(SLOTS, FF)
    weight = pl.BlockSpec((OUT_TILE, FF), lambda i: (i, 0))
    return pl.pallas_call(
        back_kernel,
        grid=(D // OUT_TILE,),
        in_specs=[act, act, act, weight, weight, weight, ANY],
        out_specs=[pl.BlockSpec((SLOTS, 2 * OUT_TILE), lambda i: (0, i)), at_zero(8, 128)],
        out_shape=[jax.ShapeDtypeStruct((SLOTS, 2 * D), BF16), TOKEN],
        compiler_params=pltpu.CompilerParams(vmem_limit_bytes=20 * MIB),
        cost_estimate=SMALL,
        name="back_pass",
    )(hidden, d_gate, d_up, gate_w, up_w, down_w, after)


def partial_kernel(at_ref, lhs_ref, rhs_ref, after_ref, *refs):
    value = dot(lhs_ref[...], rhs_ref[...], (0, 0)).astype(BF16)
    *out_refs, token_ref = refs
    for i, out_ref in enumerate(out_refs):
        if len(out_refs) == 1:
            out_ref[...] = value
        else:

            @pl.when(pl.program_id(0) // 2 == i)
            def _():
                out_ref[...] = value

    emit(token_ref)


def partial(at, rows, side, first, count, grads, column, width, after):
    def out_spec(i):
        return pl.BlockSpec(
            (CHUNK, width), lambda s, at: (jnp.clip(s - 2 * i, 0, 1) if count > 2 else s, 0)
        )

    outs = count // 2
    return pl.pallas_call(
        partial_kernel,
        grid_spec=pltpu.PrefetchScalarGridSpec(
            num_scalar_prefetch=1,
            grid=(count,),
            in_specs=[
                pl.BlockSpec((SLOTS, CHUNK), lambda s, at: (0, side * RING + at[first + s])),
                pl.BlockSpec((SLOTS, width), lambda s, at: (0, column)),
                ANY,
            ],
            out_specs=[out_spec(i) for i in range(outs)] + [at_zero(8, 128)],
        ),
        out_shape=[jax.ShapeDtypeStruct((2 * CHUNK, width), BF16)] * outs + [TOKEN],
        compiler_params=pltpu.CompilerParams(vmem_limit_bytes=12 * MIB),
        cost_estimate=SMALL,
        name="partial",
    )(at, rows, grads, after)


def split_kernel(own_ref, next_ref, got_next_ref, got_own_ref, after_ref, send_ref, keep_ref, token_ref):
    send_ref[...] = (next_ref[...].astype(F32) + got_next_ref[...].astype(F32)).astype(BF16)
    keep_ref[...] = (own_ref[...].astype(F32) + got_own_ref[...].astype(F32)).astype(BF16)
    emit(token_ref)


def split_sum(rows, own, next_, got, after):
    width = got.shape[1]

    def block(i):
        return pl.BlockSpec((rows, width), lambda s: (i, 0))

    out = jax.ShapeDtypeStruct((rows, width), BF16)
    return pl.pallas_call(
        split_kernel,
        grid=(1,),
        in_specs=[block(own[1]), block(next_[1]), block(0), block(1), ANY],
        out_specs=[block(0), block(0), at_zero(8, 128)],
        out_shape=[out, out, TOKEN],
        compiler_params=pltpu.CompilerParams(vmem_limit_bytes=16 * MIB),
        cost_estimate=STEP,
        name="split_sum",
    )(own[0], next_[0], got, got, after)


def third_kernel(at_ref, keep_ref, got_ref, after_ref, far_near_ref, next_own_ref, token_ref):
    for i in range(RING):
        rows = pl.ds(pl.multiple_of(at_ref[RING + i] * ROWS, ROWS), ROWS)
        total = (keep_ref[rows, :].astype(F32) + got_ref[rows, :].astype(F32)).astype(BF16)
        out_ref = far_near_ref if i < 2 else next_own_ref
        out_ref[i % 2 * ROWS : (i % 2 + 1) * ROWS, :] = total
    emit(token_ref)


def third_sum(at, keep, got, after, cost):
    width = keep.shape[1]
    return pl.pallas_call(
        third_kernel,
        grid_spec=pltpu.PrefetchScalarGridSpec(
            num_scalar_prefetch=1,
            grid=(1,),
            in_specs=[at_zero(CHUNK, width), at_zero(CHUNK, width), ANY],
            out_specs=[at_zero(2 * ROWS, width)] * 2 + [at_zero(8, 128)],
        ),
        out_shape=[jax.ShapeDtypeStruct((2 * ROWS, width), BF16)] * 2 + [TOKEN],
        compiler_params=pltpu.CompilerParams(vmem_limit_bytes=12 * MIB),
        cost_estimate=cost,
        name="third_sum",
    )(at, keep, got, after)


def fifth_kernel(keep_ref, got_ref, after_ref, out_ref, token_ref):
    out_ref[...] = keep_ref[...].astype(F32) + got_ref[...].astype(F32)
    emit(token_ref)


def fifth_sum(keep, got, after):
    width = keep.shape[1]
    block = at_zero(ROWS, width)
    return pl.pallas_call(
        fifth_kernel,
        grid=(1,),
        in_specs=[block, block, ANY],
        out_specs=[block, at_zero(8, 128)],
        out_shape=[jax.ShapeDtypeStruct((ROWS, width), F32), TOKEN],
        compiler_params=pltpu.CompilerParams(vmem_limit_bytes=4 * MIB),
        cost_estimate=STEP,
        name="fifth_sum",
    )(keep, got, after)


def combine_kernel(target_ref, weights_ref, back_ref, grads_ref, after_ref, mixed_ref, d_tokens_ref, d_route_ref, token_ref
):
    emit(token_ref)
    weights = weights_ref[...]
    slot = lax.broadcasted_iota(jnp.int32, (SLOTS, ROWS), 0)
    align = jnp.zeros((SLOTS, ROWS), F32)
    tiles = D // OUT_TILE
    for i in range(tiles):
        out = back_ref[:, 2 * i * OUT_TILE : (2 * i + 1) * OUT_TILE]
        align = align + dot(out, grads_ref[:, i * OUT_TILE : (i + 1) * OUT_TILE], (1, 1))
    chosen = jnp.zeros((SLOTS, ROWS), F32)
    scale = jnp.zeros((SLOTS, ROWS), F32)
    for k in range(TOP):
        here = target_ref[k : k + 1, :] == slot
        chosen = chosen + jnp.where(here, 1.0, 0.0)
        scale = scale + jnp.where(here, weights[k : k + 1, :], 0.0)
        d_route_ref[k : k + 1, :] = jnp.sum(jnp.where(here, align, 0.0), axis=0, keepdims=True)
    chosen = chosen.astype(BF16)
    high = scale.astype(BF16)
    low = (scale - high.astype(F32)).astype(BF16)
    for i in range(tiles):
        out = back_ref[:, 2 * i * OUT_TILE : (2 * i + 1) * OUT_TILE]
        d_in = back_ref[:, (2 * i + 1) * OUT_TILE : (2 * i + 2) * OUT_TILE]
        at = slice(i * OUT_TILE, (i + 1) * OUT_TILE)
        mixed_ref[:, at] = (dot(high, out, (0, 0)) + dot(low, out, (0, 0))).astype(BF16)
        d_tokens_ref[:, at] = dot(chosen, d_in, (0, 0)).astype(BF16)


def combine(target, weights, back, grads, after):
    whole = pl.BlockSpec(memory_space=pltpu.VMEM)
    return pl.pallas_call(
        combine_kernel,
        in_specs=[whole] * 4 + [ANY],
        out_shape=(
            jax.ShapeDtypeStruct((ROWS, D), BF16),
            jax.ShapeDtypeStruct((ROWS, D), BF16),
            jax.ShapeDtypeStruct((TOP, ROWS), F32),
            TOKEN,
        ),
        compiler_params=pltpu.CompilerParams(vmem_limit_bytes=20 * MIB),
        cost_estimate=SMALL,
        name="combine_rows",
    )(target, weights, back, grads, after)


def on_device(tokens, grad_out, expert_ids, route_weights, w_gate, w_up, w_down):
    x, z = lax.axis_index("dp") // RING, lax.axis_index("dp") % RING
    core = lax.axis_index("expert") % 2

    def chunk_order(at):
        beside, across = at ^ 1, RING - 1 - at
        first = jnp.where(core == 0, beside, across)
        second = jnp.where(core == 0, across, beside)
        return [(at + 2) % RING, first, second, at]

    at = jnp.stack(chunk_order(x) + chunk_order(z)).astype(jnp.int32)
    gate_w, up_w, down_w = w_gate[0], w_up[0], w_down[0]
    ids, weights = expert_ids.T, route_weights.T

    def exchange(buffer):
        buffer = buffer.reshape(EXPERTS, CAP, 2 * D)
        buffer = lax.all_to_all(buffer, "expert", split_axis=0, concat_axis=0, tiled=True)
        return buffer.reshape(SLOTS, 2 * D)

    def send_on(array, axis, stage):
        return lax.ppermute(array, ALL, pairs_of(axis, stage))

    send, target = place(at, ids, weights, tokens, grad_out)
    rows = exchange(send)
    hidden, d_gate, d_up = hidden_pass(rows, gate_w, up_w, down_w)

    factors = {"gate": (0, d_gate), "up": (0, d_up), "down": (1, hidden)}
    got, sums, grads = {}, {}, {}
    token = target
    back = None
    for step in ORDER:
        kind, name = step.split()
        if kind in ("first", "rest", "all"):
            side, factor = factors[name]
            start, count = {"first": (0, 2), "rest": (2, 2), "all": (0, 4)}[kind]
            *made, token = partial(at, rows, side, start, count, factor, 0, FF, token)
            if kind != "first":
                sums[name] = made[-1]
            if kind != "rest":
                got[name] = send_on(made[0], "x", 0)
        elif kind == "second":
            both = sums[name]
            send, sums[name], token = split_sum(CHUNK, (both, 1), (both, 0), got[name], token)
            got[name] = send_on(send, "x", 1)
        elif kind == "third":
            cost = LONG if name == "gate" else STEP
            send, sums[name], token = third_sum(at, sums[name], got[name], token, cost)
            got[name] = send_on(send, "z", 0)
        elif kind == "fourth":
            both = sums[name]
            send, sums[name], token = split_sum(ROWS, (both, 1), (both, 0), got[name], token)
            got[name] = send_on(send, "z", 1)
        elif kind == "fifth":
            total, token = fifth_sum(sums[name], got[name], token)
            grads[name] = total[None]
        elif name == "back":
            back, token = back_pass(hidden, d_gate, d_up, gate_w, up_w, down_w, token)
            back = exchange(back)
        else:
            mixed, d_tokens, d_route, token = combine(target, weights, back, grad_out, token)
    return (mixed, d_tokens, d_route.T) + tuple(grads[name] for name in ("gate", "up", "down"))


def solution(mesh):
    by_device = P(("dp", "expert"), None)
    by_expert = P("expert", None, None)
    by_row = P("expert", "dp", None)
    return jax.shard_map(
        on_device,
        mesh=mesh,
        in_specs=(by_device,) * 4 + (by_expert,) * 3,
        out_specs=(by_device,) * 3 + (by_row,) * 3,
        check_vma=False,
    )
```

time: 206 us -> 175 us (0.85)
  starting transfers between devices: 46.8 us -> 34.5 us
  Pallas kernels: 46.9 us -> 36.5 us
  local copies, waits for them, and re-layouts: 14.4 us -> 7.95 us
  other arithmetic: 2.69 us -> 0 us
    ppermute x24 -> x12, starting transfers between devices: 41.4 us -> 29.1 us  [send_on(): return lax.ppermute(array, ALL, pairs_of(axis, stage))]
    pallas_call x18, Pallas kernels: 37.2 us -> 26.8 us  [the longest x4 11.7 us: partial(): pl.pallas_call(partial_kernel, grid_spec=pltpu.PrefetchScalarGridSpec(num...]
    unnamed x48 -> x44, local copies, waits for them, and re-layouts: 14.1 us -> 7.87 us
    broadcast_in_dim x3 -> x0, other arithmetic: 2.35 us -> none  [the longest x1 0.79 us: on_device(): grad_down[None]]
    ppermute x24 -> x12, waiting for transfers between devices: 48.6 us -> 50.3 us  [send_on(): return lax.ppermute(array, ALL, pairs_of(axis, stage))]
  transfers between devices with their start and end apart: 25 -> 13, of which waited for: 12 -> 8; matrix products, arithmetic and copies ran while one was open for 1% -> 0% of each run, Pallas kernels for 15% -> 15%
where the time goes in v2:
time: 175 us; the launch traced here: 174 us
  waiting for transfers between devices  50.3 us (29%)
  blocking collectives  43.8 us (25%)
  Pallas kernels  36.5 us (21%)
  starting transfers between devices  34.5 us (20%)
  local copies, waits for them, and re-layouts  7.95 us (5%)
    ppermute x12, waiting for transfers between devices, send_on(): return lax.ppermute(array, ALL, pairs_of(axis, stage))  50.3 us
    all_to_all x1, blocking collectives, exchange(): lax.all_to_all(buffer, 'expert', split_axis=0, concat_axis=0, tiled=True)  43.8 us
    ppermute x12, starting transfers between devices, send_on(): return lax.ppermute(array, ALL, pairs_of(axis, stage))  29.1 us
    pallas_call x4, Pallas kernels, partial(): pl.pallas_call(partial_kernel, grid_spec=pltpu.PrefetchScalarGridSpec(num...  11.7 us
    unnamed x44, local copies, waits for them, and re-layouts  7.87 us
    all_to_all x1, starting transfers between devices, exchange(): lax.all_to_all(buffer, 'expert', split_axis=0, concat_axis=0, tiled=True)  5.44 us
    pallas_call x1, Pallas kernels, hidden_pass(): pl.pallas_call(hidden_kernel, grid=(FF // tile,), in_specs=[pl.BlockSpec(...  5.04 us
    pallas_call x1, Pallas kernels, back_pass(): pl.pallas_call(back_kernel, grid=(D // OUT_TILE,), in_specs=[act, act, ac...  4.65 us
  transfers between devices with their start and end apart: 13, of which 8 were waited for; matrix products, arithmetic and copies ran while one was open for 0% of the time, Pallas kernels for 15%

profile of v2, /device:TPU:32, one launch (start us, length us, event | category | flops | bytes accessed | tf_op | source)
XLA Modules:
  0.0 174.0 jit_solution(12659462139266967851)
XLA Ops:
  0.8 1.0 copy-done.10
  1.8 0.7 copy-done.12
  2.5 1.0 copy-done.14
  3.6 0.7 copy-done.15
  4.3 1.7 place_rows.1
  6.0 43.8 %all_to_all.10 = bf16[16,24,4096]{2,1,0:T(8,128)(2,1)S(1)} all-to-all(bf16[16,24,4096]{2,1,0:T(8,128)(2,1)S(1)} %bitcast.33), channel_id=1, replica_groups=mesh['dp'=16,'expert'=16] {'expert'}, dimensions={0} | all-to-all | bytes 6291456 | tf_op jit(solution)/shard_map/all_to_all | solution.py:358
  49.9 5.0 %hidden_pass.1 = (bf16[384,768]{1,0:T(8,128)(2,1)S(1)}, bf16[384,768]{1,0:T(8,128)(2,1)S(1)}, bf16[384,768]{1,0:T(8,128)(2,1)S(1)}) custom-call(bf16[384,4096]{1,0:T(8,128)(2,1)S(1)} %bitcast.21, bf16[2048,768]{1,0:T(8,128)(2,1)S(1)} %bitcast.26, bf16[2048,768]{1,0:T(8,128)(2,1)S(1)} %bitcast.28, bf16[2048,768]{1,0:T(8,128)(2,1)S(1)} %bitcast.30), custom_call_target="tpu_custom_call" | custom-call | flops 1 | bytes 1 | tf_op jit(solution)/shard_map/hidden_pass/pallas_call | solution.py:134
  54.9 2.8 %partial.4 = (bf16[1024,768]{1,0:T(8,128)(2,1)}, s32[8,128]{1,0:T(8,128)S(1)}) custom-call(s32[8]{0:T(128)S(1)} %stack.35.at_ref, bf16[384,4096]{1,0:T(8,128)(2,1)S(1)} %bitcast.22, bf16[384,768]{1,0:T(8,128)(2,1)S(1)} %get-tuple-element.62.rhs_ref.d_gate_ref, s32[6,128]{1,0:T(8,128)S(1)} %get-tuple-element.59.after_ref.target_ref), custom_call_target="tpu_custom_call" | custom-call | flops 1 | bytes 1 | tf_op jit(solution)/shard_map/partial/pallas_call | solution.py:207
  57.8 1.5 collective-permute-start
  59.3 4.6 %back_pass.1 = (bf16[384,4096]{1,0:T(8,128)(2,1)S(1)}, s32[8,128]{1,0:T(8,128)S(1)}) custom-call(bf16[384,768]{1,0:T(8,128)(2,1)S(1)} %get-tuple-element.61.hidden_ref.rhs_ref, bf16[384,768]{1,0:T(8,128)(2,1)S(1)} %get-tuple-element.62.rhs_ref.d_gate_ref, bf16[384,768]{1,0:T(8,128)(2,1)S(1)} %get-tuple-element.63.d_up_ref.rhs_ref, ...), custom_call_target="tpu_custom_call" | custom-call | flops 1 | bytes 1 | tf_op jit(solution)/shard_map/back_pass/pallas_call | solution.py:173
  63.9 1.7 copy-done.5
  65.6 5.4 %all-to-all-start.1 = ((bf16[16,24,4096]{2,1,0:T(8,128)(2,1)}), bf16[16,24,4096]{2,1,0:T(8,128)(2,1)}, u32[]{:S(2)}, u32[]{:S(2)}) async-start(bf16[16,24,4096]{2,1,0:T(8,128)(2,1)} %bitcast.32), calls=%async_computation.1 | async-start | bytes 6291456 | tf_op jit(solution)/shard_map/all_to_all | solution.py:358
  71.1 1.1 copy-done.9
  72.1 3.5 %partial.5 = (bf16[1024,768]{1,0:T(8,128)(2,1)S(1)}, bf16[1024,768]{1,0:T(8,128)(2,1)S(1)}, s32[8,128]{1,0:T(8,128)S(1)}) custom-call(s32[8]{0:T(128)S(1)} %stack.35.at_ref, bf16[384,4096]{1,0:T(8,128)(2,1)S(1)} %bitcast.23, bf16[384,768]{1,0:T(8,128)(2,1)S(1)} %copy-done.9, s32[8,128]{1,0:T(8,128)S(1)} %get-tuple-element.66.after_ref), custom_call_target="tpu_custom_call" | custom-call | flops 1 | bytes 1 | tf_op jit(solution)/shard_map/partial/pallas_call | solution.py:207
  75.6 1.9 %partial.6 = (bf16[1024,768]{1,0:T(8,128)(2,1)S(1)}, s32[8,128]{1,0:T(8,128)S(1)}) custom-call(s32[8]{0:T(128)S(1)} %stack.35.at_ref, bf16[384,4096]{1,0:T(8,128)(2,1)S(1)} %bitcast.24, bf16[384,768]{1,0:T(8,128)(2,1)S(1)} %copy-done.4, s32[8,128]{1,0:T(8,128)S(1)} %get-tuple-element.67.after_ref), custom_call_target="tpu_custom_call" | custom-call | flops 1 | bytes 1 | tf_op jit(solution)/shard_map/partial/pallas_call | solution.py:207
  77.5 1.0 collective-permute-done.got_next_ref.got_own_ref
  78.5 1.8 %split_sum.6 = (bf16[512,768]{1,0:T(8,128)(2,1)S(1)}, bf16[512,768]{1,0:T(8,128)(2,1)S(1)}, s32[8,128]{1,0:T(8,128)S(1)}) custom-call(bf16[1024,768]{1,0:T(8,128)(2,1)S(1)} %get-tuple-element.68.own_ref.next_ref, bf16[1024,768]{1,0:T(8,128)(2,1)S(1)} %get-tuple-element.68.own_ref.next_ref, bf16[1024,768]{1,0:T(8,128)(2,1)} %collective-permute-done.got_next_ref.got_own_ref, ...), custom_call_target="tpu_custom_call" | custom-call | flops 10000000000 | bytes 1 | tf_op jit(solution)/shard_map/split_sum/pallas_call | solution.py:239
  80.3 2.8 %collective-permute-start.3 = (bf16[512,768]{1,0:T(8,128)(2,1)S(1)}, bf16[512,768]{1,0:T(8,128)(2,1)S(1)}, u32[]{:S(2)}, u32[]{:S(2)}) collective-permute-start(bf16[512,768]{1,0:T(8,128)(2,1)S(1)} %get-tuple-element.77), channel_id=1, source_target_pairs={{0,192},{1,65},{2,194},{3,67},{4,196},{5,69},{6,198},{7,71},{8,200... | collective-permute-start | bytes 2359304 | tf_op jit(solution)/shard_map/ppermute | solution.py:362
  83.2 0.2 collective-permute-start.2
  83.4 3.5 %partial.7 = (bf16[1024,768]{1,0:T(8,128)(2,1)S(1)}, bf16[1024,768]{1,0:T(8,128)(2,1)S(1)}, s32[8,128]{1,0:T(8,128)S(1)}) custom-call(s32[8]{0:T(128)S(1)} %stack.35.at_ref, bf16[384,4096]{1,0:T(8,128)(2,1)S(1)} %bitcast.25, bf16[384,768]{1,0:T(8,128)(2,1)S(1)} %copy-done.7, s32[8,128]{1,0:T(8,128)S(1)} %get-tuple-element.71.after_ref), custom_call_target="tpu_custom_call" | custom-call | flops 1 | bytes 1 | tf_op jit(solution)/shard_map/partial/pallas_call | solution.py:207
  86.9 1.9 %collective-permute-start.1 = (bf16[1024,768]{1,0:T(8,128)(2,1)S(1)}, bf16[1024,768]{1,0:T(8,128)(2,1)S(1)}, u32[]{:S(2)}, u32[]{:S(2)}) collective-permute-start(bf16[1024,768]{1,0:T(8,128)(2,1)S(1)} %get-tuple-element.73), channel_id=1, source_target_pairs={{0,64},{1,193},{2,66},{3,195},{4,68},{5,197},{6,70},{7,199},{8,72}... | collective-permute-start | bytes 4718600 | tf_op jit(solution)/shard_map/ppermute | solution.py:362
  88.8 13.2 %collective-permute-done.3.got_ref = bf16[512,768]{1,0:T(8,128)(2,1)S(1)} collective-permute-done((bf16[512,768]{1,0:T(8,128)(2,1)S(1)}, bf16[512,768]{1,0:T(8,128)(2,1)S(1)}, u32[]{:S(2)}, u32[]{:S(2)}) %collective-permute-start.3) | collective-permute-done | bytes 786464 | tf_op jit(solution)/shard_map/ppermute | solution.py:362
  101.9 0.7 third_sum.3
  102.7 3.4 %collective-permute-start.5 = (bf16[256,768]{1,0:T(8,128)(2,1)S(1)}, bf16[256,768]{1,0:T(8,128)(2,1)S(1)}, u32[]{:S(2)}, u32[]{:S(2)}) collective-permute-start(bf16[256,768]{1,0:T(8,128)(2,1)S(1)} %get-tuple-element.83), channel_id=1, source_target_pairs={{0,16},{1,49},{2,18},{3,51},{4,20},{5,53},{6,22},{7,55},{8,24},{9,... | collective-permute-start | bytes 1179656 | tf_op jit(solution)/shard_map/ppermute | solution.py:362
  106.0 2.7 %collective-permute-done.2.got_next_ref.got_own_ref = bf16[1024,768]{1,0:T(8,128)(2,1)S(1)} collective-permute-done((bf16[1024,768]{1,0:T(8,128)(2,1)S(1)}, bf16[1024,768]{1,0:T(8,128)(2,1)S(1)}, u32[]{:S(2)}, u32[]{:S(2)}) %collective-permute-start.2) | collective-permute-done | bytes 1572896 | tf_op jit(solution)/shard_map/ppermute | solution.py:362
  108.7 0.4 split_sum.7
  109.1 2.8 %collective-permute-start.4 = (bf16[512,768]{1,0:T(8,128)(2,1)S(1)}, bf16[512,768]{1,0:T(8,128)(2,1)S(1)}, u32[]{:S(2)}, u32[]{:S(2)}) collective-permute-start(bf16[512,768]{1,0:T(8,128)(2,1)S(1)} %get-tuple-element.81), channel_id=1, source_target_pairs={{0,192},{1,65},{2,194},{3,67},{4,196},{5,69},{6,198},{7,71},{8,200... | collective-permute-start | bytes 2359304 | tf_op jit(solution)/shard_map/ppermute | solution.py:362
  111.9 6.9 %collective-permute-done.5.got_next_ref.got_own_ref = bf16[256,768]{1,0:T(8,128)(2,1)S(1)} collective-permute-done((bf16[256,768]{1,0:T(8,128)(2,1)S(1)}, bf16[256,768]{1,0:T(8,128)(2,1)S(1)}, u32[]{:S(2)}, u32[]{:S(2)}) %collective-permute-start.5) | collective-permute-done | bytes 393248 | tf_op jit(solution)/shard_map/ppermute | solution.py:362
  119.0 1.8 %collective-permute-start.6 = (bf16[128,768]{1,0:T(8,128)(2,1)S(1)}, bf16[128,768]{1,0:T(8,128)(2,1)}, u32[]{:S(2)}, u32[]{:S(2)}) collective-permute-start(bf16[128,768]{1,0:T(8,128)(2,1)S(1)} %get-tuple-element.92), channel_id=1, source_target_pairs={{0,48},{1,17},{2,50},{3,19},{4,52},{5,21},{6,54},{7,23},{8,56},{9,... | collective-permute-start | bytes 589832 | tf_op jit(solution)/shard_map/ppermute | solution.py:362
  120.7 10.2 %collective-permute-done.4.got_ref = bf16[512,768]{1,0:T(8,128)(2,1)S(1)} collective-permute-done((bf16[512,768]{1,0:T(8,128)(2,1)S(1)}, bf16[512,768]{1,0:T(8,128)(2,1)S(1)}, u32[]{:S(2)}, u32[]{:S(2)}) %collective-permute-start.4) | collective-permute-done | bytes 786464 | tf_op jit(solution)/shard_map/ppermute | solution.py:362
  130.9 1.4 third_sum.4
  132.3 0.7 copy-done.18
  133.0 3.3 %collective-permute-start.7 = (bf16[256,768]{1,0:T(8,128)(2,1)}, bf16[256,768]{1,0:T(8,128)(2,1)S(1)}, u32[]{:S(2)}, u32[]{:S(2)}) collective-permute-start(bf16[256,768]{1,0:T(8,128)(2,1)} %get-tuple-element.96), channel_id=1, source_target_pairs={{0,16},{1,49},{2,18},{3,51},{4,20},{5,53},{6,22},{7,55},{8,24},{9,... | collective-permute-start | bytes 1179656 | tf_op jit(solution)/shard_map/ppermute | solution.py:362
  136.3 0.4 split_sum.9
  136.7 0.9 copy-done.16
  137.5 2.8 %collective-permute-start.9 = (bf16[512,768]{1,0:T(8,128)(2,1)S(1)}, bf16[512,768]{1,0:T(8,128)(2,1)S(1)}, u32[]{:S(2)}, u32[]{:S(2)}) collective-permute-start(bf16[512,768]{1,0:T(8,128)(2,1)S(1)} %get-tuple-element.101), channel_id=1, source_target_pairs={{0,192},{1,65},{2,194},{3,67},{4,196},{5,69},{6,198},{7,71},{8,200... | collective-permute-start | bytes 2359304 | tf_op jit(solution)/shard_map/ppermute | solution.py:362
  140.3 4.5 %combine_rows.1 = (bf16[128,2048]{1,0:T(8,128)(2,1)}, bf16[128,2048]{1,0:T(8,128)(2,1)}, f32[6,128]{1,0:T(8,128)}, s32[8,128]{1,0:T(8,128)S(1)}) custom-call(s32[6,128]{1,0:T(8,128)S(1)} %get-tuple-element.59.after_ref.target_ref, f32[6,128]{1,0:T(8,128)S(1)} %bitcast.35, bf16[384,4096]{1,0:T(8,128)(2,1)} %bitcast.16.back_ref, ...), custom_call_target="tpu_custom_call" | custom-call | flops 1 | bytes 1 | tf_op jit(solution)/shard_map/combine_rows/pallas_call | solution.py:327
  144.8 1.8 %fifth_sum.3 = (f32[128,768]{1,0:T(8,128)}, s32[8,128]{1,0:T(8,128)S(1)}) custom-call(bf16[128,768]{1,0:T(8,128)(2,1)S(1)} %copy-done.21, bf16[128,768]{1,0:T(8,128)(2,1)} %collective-permute-done.6.got_ref, s32[8,128]{1,0:T(8,128)S(1)} %get-tuple-element.93.after_ref), custom_call_target="tpu_custom_call" | custom-call | flops 10000000000 | bytes 1 | tf_op jit(solution)/shard_map/fifth_sum/pallas_call | solution.py:285
  146.6 0.1 split_sum.10
  146.7 4.9 %collective-permute-start.8 = (bf16[128,768]{1,0:T(8,128)(2,1)S(1)}, bf16[128,768]{1,0:T(8,128)(2,1)S(1)}, u32[]{:S(2)}, u32[]{:S(2)}) collective-permute-start(bf16[128,768]{1,0:T(8,128)(2,1)S(1)} %get-tuple-element.99), channel_id=1, source_target_pairs={{0,48},{1,17},{2,50},{3,19},{4,52},{5,21},{6,54},{7,23},{8,56},{9,... | collective-permute-start | bytes 589832 | tf_op jit(solution)/shard_map/ppermute | solution.py:362
  151.6 0.7 third_sum.5
  152.3 0.9 collective-permute-start.10
  153.3 8.5 %collective-permute-done.8.got_ref = bf16[128,768]{1,0:T(8,128)(2,1)S(1)} collective-permute-done((bf16[128,768]{1,0:T(8,128)(2,1)S(1)}, bf16[128,768]{1,0:T(8,128)(2,1)S(1)}, u32[]{:S(2)}, u32[]{:S(2)}) %collective-permute-start.8) | collective-permute-done | bytes 196640 | tf_op jit(solution)/shard_map/ppermute | solution.py:362
  161.8 0.8 fifth_sum.4
  162.6 2.7 %collective-permute-done.10.got_next_ref.got_own_ref = bf16[256,768]{1,0:T(8,128)(2,1)S(1)} collective-permute-done((bf16[256,768]{1,0:T(8,128)(2,1)S(1)}, bf16[256,768]{1,0:T(8,128)(2,1)S(1)}, u32[]{:S(2)}, u32[]{:S(2)}) %collective-permute-start.10) | collective-permute-done | bytes 393248 | tf_op jit(solution)/shard_map/ppermute | solution.py:362
  165.4 2.8 %collective-permute-start.11 = (bf16[128,768]{1,0:T(8,128)(2,1)S(1)}, bf16[128,768]{1,0:T(8,128)(2,1)S(1)}, u32[]{:S(2)}, u32[]{:S(2)}) collective-permute-start(bf16[128,768]{1,0:T(8,128)(2,1)S(1)} %get-tuple-element.109), channel_id=1, source_target_pairs={{0,48},{1,17},{2,50},{3,19},{4,52},{5,21},{6,54},{7,23},{8,56},{9,... | collective-permute-start | bytes 589832 | tf_op jit(solution)/shard_map/ppermute | solution.py:362
  168.2 5.1 %collective-permute-done.11.got_ref = bf16[128,768]{1,0:T(8,128)(2,1)S(1)} collective-permute-done((bf16[128,768]{1,0:T(8,128)(2,1)S(1)}, bf16[128,768]{1,0:T(8,128)(2,1)S(1)}, u32[]{:S(2)}, u32[]{:S(2)}) %collective-permute-start.11) | collective-permute-done | bytes 196640 | tf_op jit(solution)/shard_map/ppermute | solution.py:362
  173.2 0.8 fifth_sum.5
  (44 shorter events, 0.4 us)
Async XLA Ops:
  0.8 1.0 copy-start.10
  1.8 0.7 copy-start.12
  2.5 1.0 copy-start.14
  3.6 0.7 copy-start.15
  4.3 45.6 %copy-start.2 = (bf16[1,2048,768]{2,1,0:T(8,128)(2,1)S(1)}, bf16[1,2048,768]{2,1,0:T(8,128)(2,1)}, u32[]{:S(2)}) copy-start(bf16[1,2048,768]{2,1,0:T(8,128)(2,1)} %param.13) | copy-start | bytes 9437188
  6.0 43.9 %copy-start = (bf16[1,2048,768]{2,1,0:T(8,128)(2,1)S(1)}, bf16[1,2048,768]{2,1,0:T(8,128)(2,1)}, u32[]{:S(2)}) copy-start(bf16[1,2048,768]{2,1,0:T(8,128)(2,1)} %param.11) | copy-start | bytes 9437188
  6.0 43.8 %copy-start.1 = (bf16[1,2048,768]{2,1,0:T(8,128)(2,1)S(1)}, bf16[1,2048,768]{2,1,0:T(8,128)(2,1)}, u32[]{:S(2)}) copy-start(bf16[1,2048,768]{2,1,0:T(8,128)(2,1)} %param.12) | copy-start | bytes 9437188
  54.9 4.4 %copy-start.3 = (bf16[384,768]{1,0:T(8,128)(2,1)}, bf16[384,768]{1,0:T(8,128)(2,1)S(1)}, u32[]{:S(2)}) copy-start(bf16[384,768]{1,0:T(8,128)(2,1)S(1)} %get-tuple-element.62.rhs_ref.d_gate_ref) | copy-start | bytes 1769476
  54.9 4.4 %copy-start.6 = (bf16[384,768]{1,0:T(8,128)(2,1)}, bf16[384,768]{1,0:T(8,128)(2,1)S(1)}, u32[]{:S(2)}) copy-start(bf16[384,768]{1,0:T(8,128)(2,1)S(1)} %get-tuple-element.61.hidden_ref.rhs_ref) | copy-start | bytes 1769476
  54.9 4.4 %copy-start.8 = (bf16[384,768]{1,0:T(8,128)(2,1)}, bf16[384,768]{1,0:T(8,128)(2,1)S(1)}, u32[]{:S(2)}) copy-start(bf16[384,768]{1,0:T(8,128)(2,1)S(1)} %get-tuple-element.63.d_up_ref.rhs_ref) | copy-start | bytes 1769476
  57.8 20.7 %collective-permute-start = (bf16[1024,768]{1,0:T(8,128)(2,1)}, bf16[1024,768]{1,0:T(8,128)(2,1)}, u32[]{:S(2)}, u32[]{:S(2)}) collective-permute-start(bf16[1024,768]{1,0:T(8,128)(2,1)} %get-tuple-element.69), channel_id=1, source_target_pairs={{0,64},{1,193},{2,66},{3,195},{4,68},{5,197},{6,70},{7,199},{8,72}... | collective-permute-start | bytes 4718600 | tf_op jit(solution)/shard_map/ppermute | solution.py:362
  63.9 1.7 copy-start.5
  65.6 74.7 %all-to-all-start.1 = ((bf16[16,24,4096]{2,1,0:T(8,128)(2,1)}), bf16[16,24,4096]{2,1,0:T(8,128)(2,1)}, u32[]{:S(2)}, u32[]{:S(2)}) async-start(bf16[16,24,4096]{2,1,0:T(8,128)(2,1)} %bitcast.32), calls=%async_computation.1 | async-start | bytes 6291456 | tf_op jit(solution)/shard_map/all_to_all | solution.py:358
  71.1 1.1 copy-start.9
  72.1 3.5 %copy-start.4 = (bf16[384,768]{1,0:T(8,128)(2,1)S(1)}, bf16[384,768]{1,0:T(8,128)(2,1)}, u32[]{:S(2)}) copy-start(bf16[384,768]{1,0:T(8,128)(2,1)} %copy-done.3) | copy-start | bytes 1769476
  78.5 4.9 %copy-start.7 = (bf16[384,768]{1,0:T(8,128)(2,1)S(1)}, bf16[384,768]{1,0:T(8,128)(2,1)}, u32[]{:S(2)}) copy-start(bf16[384,768]{1,0:T(8,128)(2,1)} %copy-done.6) | copy-start | bytes 1769476
  80.3 21.6 %collective-permute-start.3 = (bf16[512,768]{1,0:T(8,128)(2,1)S(1)}, bf16[512,768]{1,0:T(8,128)(2,1)S(1)}, u32[]{:S(2)}, u32[]{:S(2)}) collective-permute-start(bf16[512,768]{1,0:T(8,128)(2,1)S(1)} %get-tuple-element.77), channel_id=1, source_target_pairs={{0,192},{1,65},{2,194},{3,67},{4,196},{5,69},{6,198},{7,71},{8,200... | collective-permute-start | bytes 2359304 | tf_op jit(solution)/shard_map/ppermute | solution.py:362
  83.2 25.6 %collective-permute-start.2 = (bf16[1024,768]{1,0:T(8,128)(2,1)S(1)}, bf16[1024,768]{1,0:T(8,128)(2,1)S(1)}, u32[]{:S(2)}, u32[]{:S(2)}) collective-permute-start(bf16[1024,768]{1,0:T(8,128)(2,1)S(1)} %get-tuple-element.75), channel_id=1, source_target_pairs={{0,64},{1,193},{2,66},{3,195},{4,68},{5,197},{6,70},{7,199},{8,72}... | collective-permute-start | bytes 4718600 | tf_op jit(solution)/shard_map/ppermute | solution.py:362
  86.9 49.4 %collective-permute-start.1 = (bf16[1024,768]{1,0:T(8,128)(2,1)S(1)}, bf16[1024,768]{1,0:T(8,128)(2,1)S(1)}, u32[]{:S(2)}, u32[]{:S(2)}) collective-permute-start(bf16[1024,768]{1,0:T(8,128)(2,1)S(1)} %get-tuple-element.73), channel_id=1, source_target_pairs={{0,64},{1,193},{2,66},{3,195},{4,68},{5,197},{6,70},{7,199},{8,72}... | collective-permute-start | bytes 4718600 | tf_op jit(solution)/shard_map/ppermute | solution.py:362
  102.7 16.2 %collective-permute-start.5 = (bf16[256,768]{1,0:T(8,128)(2,1)S(1)}, bf16[256,768]{1,0:T(8,128)(2,1)S(1)}, u32[]{:S(2)}, u32[]{:S(2)}) collective-permute-start(bf16[256,768]{1,0:T(8,128)(2,1)S(1)} %get-tuple-element.83), channel_id=1, source_target_pairs={{0,16},{1,49},{2,18},{3,51},{4,20},{5,53},{6,22},{7,55},{8,24},{9,... | collective-permute-start | bytes 1179656 | tf_op jit(solution)/shard_map/ppermute | solution.py:362
  109.1 21.8 %collective-permute-start.4 = (bf16[512,768]{1,0:T(8,128)(2,1)S(1)}, bf16[512,768]{1,0:T(8,128)(2,1)S(1)}, u32[]{:S(2)}, u32[]{:S(2)}) collective-permute-start(bf16[512,768]{1,0:T(8,128)(2,1)S(1)} %get-tuple-element.81), channel_id=1, source_target_pairs={{0,192},{1,65},{2,194},{3,67},{4,196},{5,69},{6,198},{7,71},{8,200... | collective-permute-start | bytes 2359304 | tf_op jit(solution)/shard_map/ppermute | solution.py:362
  119.0 13.3 %copy-start.20 = (bf16[128,768]{1,0:T(8,128)(2,1)}, bf16[128,768]{1,0:T(8,128)(2,1)S(1)}, u32[]{:S(2)}) copy-start(bf16[128,768]{1,0:T(8,128)(2,1)S(1)} %get-tuple-element.91.keep_ref) | copy-start | bytes 589828
  119.0 25.8 %collective-permute-start.6 = (bf16[128,768]{1,0:T(8,128)(2,1)S(1)}, bf16[128,768]{1,0:T(8,128)(2,1)}, u32[]{:S(2)}, u32[]{:S(2)}) collective-permute-start(bf16[128,768]{1,0:T(8,128)(2,1)S(1)} %get-tuple-element.92), channel_id=1, source_target_pairs={{0,48},{1,17},{2,50},{3,19},{4,52},{5,21},{6,54},{7,23},{8,56},{9,... | collective-permute-start | bytes 589832 | tf_op jit(solution)/shard_map/ppermute | solution.py:362
  132.3 0.7 copy-start.18
  133.0 13.6 %collective-permute-start.7 = (bf16[256,768]{1,0:T(8,128)(2,1)}, bf16[256,768]{1,0:T(8,128)(2,1)S(1)}, u32[]{:S(2)}, u32[]{:S(2)}) collective-permute-start(bf16[256,768]{1,0:T(8,128)(2,1)} %get-tuple-element.96), channel_id=1, source_target_pairs={{0,16},{1,49},{2,18},{3,51},{4,20},{5,53},{6,22},{7,55},{8,24},{9,... | collective-permute-start | bytes 1179656 | tf_op jit(solution)/shard_map/ppermute | solution.py:362
  136.3 4.0 %copy-start.11 = (bf16[128,2048]{1,0:T(8,128)(2,1)S(1)}, bf16[128,2048]{1,0:T(8,128)(2,1)}, u32[]{:S(2)}) copy-start(bf16[128,2048]{1,0:T(8,128)(2,1)} %grads_ref.3) | copy-start | bytes 1572868
  136.3 4.0 %copy-start.13 = (f32[128,6]{0,1:T(8,128)S(1)}, f32[128,6]{0,1:T(8,128)}, u32[]{:S(2)}) copy-start(f32[128,6]{0,1:T(8,128)} %param.10) | copy-start | bytes 9220
  136.7 0.9 copy-start.16
  137.5 14.1 %collective-permute-start.9 = (bf16[512,768]{1,0:T(8,128)(2,1)S(1)}, bf16[512,768]{1,0:T(8,128)(2,1)S(1)}, u32[]{:S(2)}, u32[]{:S(2)}) collective-permute-start(bf16[512,768]{1,0:T(8,128)(2,1)S(1)} %get-tuple-element.101), channel_id=1, source_target_pairs={{0,192},{1,65},{2,194},{3,67},{4,196},{5,69},{6,198},{7,71},{8,200... | collective-permute-start | bytes 2359304 | tf_op jit(solution)/shard_map/ppermute | solution.py:362
  140.3 4.5 %copy-start.21 = (bf16[128,768]{1,0:T(8,128)(2,1)S(1)}, bf16[128,768]{1,0:T(8,128)(2,1)}, u32[]{:S(2)}) copy-start(bf16[128,768]{1,0:T(8,128)(2,1)} %copy-done.20) | copy-start | bytes 589828
  144.8 1.8 %copy-start.19 = (bf16[256,768]{1,0:T(8,128)(2,1)S(1)}, bf16[256,768]{1,0:T(8,128)(2,1)}, u32[]{:S(2)}) copy-start(bf16[256,768]{1,0:T(8,128)(2,1)} %copy-done.18) | copy-start | bytes 1179652
  146.6 5.0 %copy-start.17 = (bf16[512,768]{1,0:T(8,128)(2,1)S(1)}, bf16[512,768]{1,0:T(8,128)(2,1)}, u32[]{:S(2)}) copy-start(bf16[512,768]{1,0:T(8,128)(2,1)} %copy-done.16) | copy-start | bytes 2359300
  146.7 15.1 %collective-permute-start.8 = (bf16[128,768]{1,0:T(8,128)(2,1)S(1)}, bf16[128,768]{1,0:T(8,128)(2,1)S(1)}, u32[]{:S(2)}, u32[]{:S(2)}) collective-permute-start(bf16[128,768]{1,0:T(8,128)(2,1)S(1)} %get-tuple-element.99), channel_id=1, source_target_pairs={{0,48},{1,17},{2,50},{3,19},{4,52},{5,21},{6,54},{7,23},{8,56},{9,... | collective-permute-start | bytes 589832 | tf_op jit(solution)/shard_map/ppermute | solution.py:362
  152.3 12.9 %collective-permute-start.10 = (bf16[256,768]{1,0:T(8,128)(2,1)S(1)}, bf16[256,768]{1,0:T(8,128)(2,1)S(1)}, u32[]{:S(2)}, u32[]{:S(2)}) collective-permute-start(bf16[256,768]{1,0:T(8,128)(2,1)S(1)} %get-tuple-element.106), channel_id=1, source_target_pairs={{0,16},{1,49},{2,18},{3,51},{4,20},{5,53},{6,22},{7,55},{8,24},{9,... | collective-permute-start | bytes 1179656 | tf_op jit(solution)/shard_map/ppermute | solution.py:362
  165.4 7.9 %collective-permute-start.11 = (bf16[128,768]{1,0:T(8,128)(2,1)S(1)}, bf16[128,768]{1,0:T(8,128)(2,1)S(1)}, u32[]{:S(2)}, u32[]{:S(2)}) collective-permute-start(bf16[128,768]{1,0:T(8,128)(2,1)S(1)} %get-tuple-element.109), channel_id=1, source_target_pairs={{0,48},{1,17},{2,50},{3,19},{4,52},{5,21},{6,54},{7,23},{8,56},{9,... | collective-permute-start | bytes 589832 | tf_op jit(solution)/shard_map/ppermute | solution.py:362

commit v3 on v2

--- a/solution.py
+++ b/solution.py
@@ -14,8 +14,8 @@
 FF = 768
 RING = 4
 MIB = 1024 * 1024
-LONG = pl.CostEstimate(flops=10**10, bytes_accessed=MIB, transcendentals=0)
-STEP = pl.CostEstimate(flops=10**10, bytes_accessed=1, transcendentals=0)
+LONG = pl.CostEstimate(flops=6 * 10**9, bytes_accessed=MIB, transcendentals=0)
+STEP = pl.CostEstimate(flops=6 * 10**9, bytes_accessed=1, transcendentals=0)
 SMALL = pl.CostEstimate(flops=1, bytes_accessed=1, transcendentals=0)
 F32 = jnp.float32
 BF16 = jnp.bfloat16
@@ -32,10 +32,10 @@
     "fourth gate",
     "third up",
     "second down",
-    "run combine",
     "fifth gate",
     "fourth up",
     "third down",
+    "run combine",
     "fifth up",
     "fourth down",
     "fifth down",

time: 175 us -> 174 us (level)
  waiting for transfers between devices: 50.3 us -> 55.5 us
  starting transfers between devices: 34.5 us -> 32.2 us
    ppermute x12, waiting for transfers between devices: 50.3 us -> 55.5 us  [send_on(): return lax.ppermute(array, ALL, pairs_of(axis, stage))]
    ppermute x12, starting transfers between devices: 29.1 us -> 26.8 us  [send_on(): return lax.ppermute(array, ALL, pairs_of(axis, stage))]
    unnamed x44 -> x32, local copies, waits for them, and re-layouts: 7.87 us -> 6.23 us
  transfers between devices with their start and end apart: 13 -> 13, of which waited for: 8 -> 9; matrix products, arithmetic and copies ran while one was open for 0% -> 0% of each run, Pallas kernels for 15% -> 14%
where the time goes in v3:
time: 174 us
  waiting for transfers between devices  55.5 us (32%)
  blocking collectives  43.8 us (25%)
  Pallas kernels  34.8 us (20%)
  starting transfers between devices  32.2 us (19%)
  local copies, waits for them, and re-layouts  6.32 us (4%)
    ppermute x12, waiting for transfers between devices, send_on(): return lax.ppermute(array, ALL, pairs_of(axis, stage))  55.5 us
    all_to_all x1, blocking collectives, exchange(): lax.all_to_all(buffer, 'expert', split_axis=0, concat_axis=0, tiled=True)  43.8 us
    ppermute x12, starting transfers between devices, send_on(): return lax.ppermute(array, ALL, pairs_of(axis, stage))  26.8 us
    pallas_call x4, Pallas kernels, partial(): pl.pallas_call(partial_kernel, grid_spec=pltpu.PrefetchScalarGridSpec(num...  11.6 us
    unnamed x32, local copies, waits for them, and re-layouts  6.23 us
    all_to_all x1, starting transfers between devices, exchange(): lax.all_to_all(buffer, 'expert', split_axis=0, concat_axis=0, tiled=True)  5.45 us
    pallas_call x1, Pallas kernels, hidden_pass(): pl.pallas_call(hidden_kernel, grid=(FF // tile,), in_specs=[pl.BlockSpec(...  5.04 us
    pallas_call x1, Pallas kernels, back_pass(): pl.pallas_call(back_kernel, grid=(D // OUT_TILE,), in_specs=[act, act, ac...  4.65 us
  transfers between devices with their start and end apart: 13, of which 9 were waited for; matrix products, arithmetic and copies ran while one was open for 0% of the time, Pallas kernels for 14%

profile of v3, /device:TPU:32, one launch (start us, length us, event | category | flops | bytes accessed | tf_op | source)
XLA Modules:
  0.0 173.6 jit_solution(1320423419000037255)
XLA Ops:
  0.8 1.0 copy-done.10
  1.8 0.7 copy-done.12
  2.5 1.0 copy-done.14
  3.6 0.7 copy-done.15
  4.3 1.7 place_rows.1
  6.0 43.8 %all_to_all.10 = bf16[16,24,4096]{2,1,0:T(8,128)(2,1)S(1)} all-to-all(bf16[16,24,4096]{2,1,0:T(8,128)(2,1)S(1)} %bitcast.33), channel_id=1, replica_groups=mesh['dp'=16,'expert'=16] {'expert'}, dimensions={0} | all-to-all | bytes 6291456 | tf_op jit(solution)/shard_map/all_to_all | solution.py:358
  49.9 5.0 %hidden_pass.1 = (bf16[384,768]{1,0:T(8,128)(2,1)S(1)}, bf16[384,768]{1,0:T(8,128)(2,1)S(1)}, bf16[384,768]{1,0:T(8,128)(2,1)S(1)}) custom-call(bf16[384,4096]{1,0:T(8,128)(2,1)S(1)} %bitcast.21, bf16[2048,768]{1,0:T(8,128)(2,1)S(1)} %bitcast.26, bf16[2048,768]{1,0:T(8,128)(2,1)S(1)} %bitcast.28, bf16[2048,768]{1,0:T(8,128)(2,1)S(1)} %bitcast.30), custom_call_target="tpu_custom_call" | custom-call | flops 1 | bytes 1 | tf_op jit(solution)/shard_map/hidden_pass/pallas_call | solution.py:134
  54.9 2.8 %partial.4 = (bf16[1024,768]{1,0:T(8,128)(2,1)}, s32[8,128]{1,0:T(8,128)S(1)}) custom-call(s32[8]{0:T(128)S(1)} %stack.35.at_ref, bf16[384,4096]{1,0:T(8,128)(2,1)S(1)} %bitcast.22, bf16[384,768]{1,0:T(8,128)(2,1)S(1)} %get-tuple-element.62.rhs_ref.d_gate_ref, s32[6,128]{1,0:T(8,128)S(1)} %get-tuple-element.59.after_ref.target_ref), custom_call_target="tpu_custom_call" | custom-call | flops 1 | bytes 1 | tf_op jit(solution)/shard_map/partial/pallas_call | solution.py:207
  57.8 1.5 collective-permute-start
  59.3 4.6 %back_pass.1 = (bf16[384,4096]{1,0:T(8,128)(2,1)S(1)}, s32[8,128]{1,0:T(8,128)S(1)}) custom-call(bf16[384,768]{1,0:T(8,128)(2,1)S(1)} %get-tuple-element.61.hidden_ref.rhs_ref, bf16[384,768]{1,0:T(8,128)(2,1)S(1)} %get-tuple-element.62.rhs_ref.d_gate_ref, bf16[384,768]{1,0:T(8,128)(2,1)S(1)} %get-tuple-element.63.d_up_ref.rhs_ref, ...), custom_call_target="tpu_custom_call" | custom-call | flops 1 | bytes 1 | tf_op jit(solution)/shard_map/back_pass/pallas_call | solution.py:173
  63.9 1.7 copy-done.5
  65.6 5.5 %all-to-all-start.1 = ((bf16[16,24,4096]{2,1,0:T(8,128)(2,1)}), bf16[16,24,4096]{2,1,0:T(8,128)(2,1)}, u32[]{:S(2)}, u32[]{:S(2)}) async-start(bf16[16,24,4096]{2,1,0:T(8,128)(2,1)} %bitcast.32), calls=%async_computation.1 | async-start | bytes 6291456 | tf_op jit(solution)/shard_map/all_to_all | solution.py:358
  71.1 1.1 copy-done.9
  72.1 3.5 %partial.5 = (bf16[1024,768]{1,0:T(8,128)(2,1)S(1)}, bf16[1024,768]{1,0:T(8,128)(2,1)S(1)}, s32[8,128]{1,0:T(8,128)S(1)}) custom-call(s32[8]{0:T(128)S(1)} %stack.35.at_ref, bf16[384,4096]{1,0:T(8,128)(2,1)S(1)} %bitcast.23, bf16[384,768]{1,0:T(8,128)(2,1)S(1)} %copy-done.9, s32[8,128]{1,0:T(8,128)S(1)} %get-tuple-element.66.after_ref), custom_call_target="tpu_custom_call" | custom-call | flops 1 | bytes 1 | tf_op jit(solution)/shard_map/partial/pallas_call | solution.py:207
  75.6 1.9 %partial.6 = (bf16[1024,768]{1,0:T(8,128)(2,1)S(1)}, s32[8,128]{1,0:T(8,128)S(1)}) custom-call(s32[8]{0:T(128)S(1)} %stack.35.at_ref, bf16[384,4096]{1,0:T(8,128)(2,1)S(1)} %bitcast.24, bf16[384,768]{1,0:T(8,128)(2,1)S(1)} %copy-done.4, s32[8,128]{1,0:T(8,128)S(1)} %get-tuple-element.67.after_ref), custom_call_target="tpu_custom_call" | custom-call | flops 1 | bytes 1 | tf_op jit(solution)/shard_map/partial/pallas_call | solution.py:207
  77.5 0.7 collective-permute-start.2
  78.1 0.3 collective-permute-done.got_next_ref.got_own_ref
  78.5 1.8 %split_sum.6 = (bf16[512,768]{1,0:T(8,128)(2,1)S(1)}, bf16[512,768]{1,0:T(8,128)(2,1)S(1)}, s32[8,128]{1,0:T(8,128)S(1)}) custom-call(bf16[1024,768]{1,0:T(8,128)(2,1)S(1)} %get-tuple-element.68.own_ref.next_ref, bf16[1024,768]{1,0:T(8,128)(2,1)S(1)} %get-tuple-element.68.own_ref.next_ref, bf16[1024,768]{1,0:T(8,128)(2,1)} %collective-permute-done.got_next_ref.got_own_ref, ...), custom_call_target="tpu_custom_call" | custom-call | flops 6000000000 | bytes 1 | tf_op jit(solution)/shard_map/split_sum/pallas_call | solution.py:239
  80.3 2.8 %collective-permute-start.3 = (bf16[512,768]{1,0:T(8,128)(2,1)S(1)}, bf16[512,768]{1,0:T(8,128)(2,1)S(1)}, u32[]{:S(2)}, u32[]{:S(2)}) collective-permute-start(bf16[512,768]{1,0:T(8,128)(2,1)S(1)} %get-tuple-element.77), channel_id=1, source_target_pairs={{0,192},{1,65},{2,194},{3,67},{4,196},{5,69},{6,198},{7,71},{8,200... | collective-permute-start | bytes 2359304 | tf_op jit(solution)/shard_map/ppermute | solution.py:362
  83.1 3.5 %partial.7 = (bf16[1024,768]{1,0:T(8,128)(2,1)S(1)}, bf16[1024,768]{1,0:T(8,128)(2,1)S(1)}, s32[8,128]{1,0:T(8,128)S(1)}) custom-call(s32[8]{0:T(128)S(1)} %stack.35.at_ref, bf16[384,4096]{1,0:T(8,128)(2,1)S(1)} %bitcast.25, bf16[384,768]{1,0:T(8,128)(2,1)S(1)} %copy-done.7, s32[8,128]{1,0:T(8,128)S(1)} %get-tuple-element.71.after_ref), custom_call_target="tpu_custom_call" | custom-call | flops 1 | bytes 1 | tf_op jit(solution)/shard_map/partial/pallas_call | solution.py:207
  86.6 0.3 collective-permute-start.1
  86.9 15.1 %collective-permute-done.3.got_ref = bf16[512,768]{1,0:T(8,128)(2,1)S(1)} collective-permute-done((bf16[512,768]{1,0:T(8,128)(2,1)S(1)}, bf16[512,768]{1,0:T(8,128)(2,1)S(1)}, u32[]{:S(2)}, u32[]{:S(2)}) %collective-permute-start.3) | collective-permute-done | bytes 786464 | tf_op jit(solution)/shard_map/ppermute | solution.py:362
  102.1 0.7 third_sum.3
  102.8 3.4 %collective-permute-start.5 = (bf16[256,768]{1,0:T(8,128)(2,1)S(1)}, bf16[256,768]{1,0:T(8,128)(2,1)S(1)}, u32[]{:S(2)}, u32[]{:S(2)}) collective-permute-start(bf16[256,768]{1,0:T(8,128)(2,1)S(1)} %get-tuple-element.83), channel_id=1, source_target_pairs={{0,16},{1,49},{2,18},{3,51},{4,20},{5,53},{6,22},{7,55},{8,24},{9,... | collective-permute-start | bytes 1179656 | tf_op jit(solution)/shard_map/ppermute | solution.py:362
  106.2 0.3 collective-permute-done.2.got_next_ref.got_own_ref
  106.4 0.4 split_sum.7
  106.8 2.6 %collective-permute-start.4 = (bf16[512,768]{1,0:T(8,128)(2,1)S(1)}, bf16[512,768]{1,0:T(8,128)(2,1)S(1)}, u32[]{:S(2)}, u32[]{:S(2)}) collective-permute-start(bf16[512,768]{1,0:T(8,128)(2,1)S(1)} %get-tuple-element.81), channel_id=1, source_target_pairs={{0,192},{1,65},{2,194},{3,67},{4,196},{5,69},{6,198},{7,71},{8,200... | collective-permute-start | bytes 2359304 | tf_op jit(solution)/shard_map/ppermute | solution.py:362
  109.4 9.5 %collective-permute-done.5.got_next_ref.got_own_ref = bf16[256,768]{1,0:T(8,128)(2,1)S(1)} collective-permute-done((bf16[256,768]{1,0:T(8,128)(2,1)S(1)}, bf16[256,768]{1,0:T(8,128)(2,1)S(1)}, u32[]{:S(2)}, u32[]{:S(2)}) %collective-permute-start.5) | collective-permute-done | bytes 393248 | tf_op jit(solution)/shard_map/ppermute | solution.py:362
  118.8 0.1 split_sum.8
  118.9 1.8 %collective-permute-start.8 = (bf16[128,768]{1,0:T(8,128)(2,1)S(1)}, bf16[128,768]{1,0:T(8,128)(2,1)S(1)}, u32[]{:S(2)}, u32[]{:S(2)}) collective-permute-start(bf16[128,768]{1,0:T(8,128)(2,1)S(1)} %get-tuple-element.92), channel_id=1, source_target_pairs={{0,48},{1,17},{2,50},{3,19},{4,52},{5,21},{6,54},{7,23},{8,56},{9,... | collective-permute-start | bytes 589832 | tf_op jit(solution)/shard_map/ppermute | solution.py:362
  120.7 7.9 %collective-permute-done.4.got_ref = bf16[512,768]{1,0:T(8,128)(2,1)S(1)} collective-permute-done((bf16[512,768]{1,0:T(8,128)(2,1)S(1)}, bf16[512,768]{1,0:T(8,128)(2,1)S(1)}, u32[]{:S(2)}, u32[]{:S(2)}) %collective-permute-start.4) | collective-permute-done | bytes 786464 | tf_op jit(solution)/shard_map/ppermute | solution.py:362
  128.6 0.7 third_sum.4
  129.3 3.5 %collective-permute-start.7 = (bf16[256,768]{1,0:T(8,128)(2,1)S(1)}, bf16[256,768]{1,0:T(8,128)(2,1)S(1)}, u32[]{:S(2)}, u32[]{:S(2)}) collective-permute-start(bf16[256,768]{1,0:T(8,128)(2,1)S(1)} %get-tuple-element.90), channel_id=1, source_target_pairs={{0,16},{1,49},{2,18},{3,51},{4,20},{5,53},{6,22},{7,55},{8,24},{9,... | collective-permute-start | bytes 1179656 | tf_op jit(solution)/shard_map/ppermute | solution.py:362
  132.8 0.4 split_sum.9
  133.2 2.2 %collective-permute-start.6 = (bf16[512,768]{1,0:T(8,128)(2,1)S(1)}, bf16[512,768]{1,0:T(8,128)(2,1)S(1)}, u32[]{:S(2)}, u32[]{:S(2)}) collective-permute-start(bf16[512,768]{1,0:T(8,128)(2,1)S(1)} %get-tuple-element.88), channel_id=1, source_target_pairs={{0,192},{1,65},{2,194},{3,67},{4,196},{5,69},{6,198},{7,71},{8,200... | collective-permute-start | bytes 2359304 | tf_op jit(solution)/shard_map/ppermute | solution.py:362
  135.4 0.8 fifth_sum.3
  136.2 5.9 %collective-permute-done.7.got_next_ref.got_own_ref = bf16[256,768]{1,0:T(8,128)(2,1)S(1)} collective-permute-done((bf16[256,768]{1,0:T(8,128)(2,1)S(1)}, bf16[256,768]{1,0:T(8,128)(2,1)S(1)}, u32[]{:S(2)}, u32[]{:S(2)}) %collective-permute-start.7) | collective-permute-done | bytes 393248 | tf_op jit(solution)/shard_map/ppermute | solution.py:362
  142.0 0.1 split_sum.10
  142.1 5.5 %collective-permute-start.9 = (bf16[128,768]{1,0:T(8,128)(2,1)S(1)}, bf16[128,768]{1,0:T(8,128)(2,1)S(1)}, u32[]{:S(2)}, u32[]{:S(2)}) collective-permute-start(bf16[128,768]{1,0:T(8,128)(2,1)S(1)} %get-tuple-element.102), channel_id=1, source_target_pairs={{0,48},{1,17},{2,50},{3,19},{4,52},{5,21},{6,54},{7,23},{8,56},{9,... | collective-permute-start | bytes 589832 | tf_op jit(solution)/shard_map/ppermute | solution.py:362
  147.6 0.7 third_sum.5
  148.4 1.1 collective-permute-start.10
  149.5 4.4 %combine_rows.1 = (bf16[128,2048]{1,0:T(8,128)(2,1)}, bf16[128,2048]{1,0:T(8,128)(2,1)}, f32[6,128]{1,0:T(8,128)}, s32[8,128]{1,0:T(8,128)S(1)}) custom-call(s32[6,128]{1,0:T(8,128)S(1)} %get-tuple-element.59.after_ref.target_ref, f32[6,128]{1,0:T(8,128)S(1)} %bitcast.35, bf16[384,4096]{1,0:T(8,128)(2,1)} %bitcast.16.back_ref, ...), custom_call_target="tpu_custom_call" | custom-call | flops 1 | bytes 1 | tf_op jit(solution)/shard_map/combine_rows/pallas_call | solution.py:327
  153.9 5.6 %collective-permute-done.9.got_ref = bf16[128,768]{1,0:T(8,128)(2,1)S(1)} collective-permute-done((bf16[128,768]{1,0:T(8,128)(2,1)S(1)}, bf16[128,768]{1,0:T(8,128)(2,1)S(1)}, u32[]{:S(2)}, u32[]{:S(2)}) %collective-permute-start.9) | collective-permute-done | bytes 196640 | tf_op jit(solution)/shard_map/ppermute | solution.py:362
  159.5 0.8 fifth_sum.4
  160.3 2.6 %collective-permute-done.10.got_next_ref.got_own_ref = bf16[256,768]{1,0:T(8,128)(2,1)S(1)} collective-permute-done((bf16[256,768]{1,0:T(8,128)(2,1)S(1)}, bf16[256,768]{1,0:T(8,128)(2,1)S(1)}, u32[]{:S(2)}, u32[]{:S(2)}) %collective-permute-start.10) | collective-permute-done | bytes 393248 | tf_op jit(solution)/shard_map/ppermute | solution.py:362
  162.9 1.4 collective-permute-start.11
  164.4 8.4 %collective-permute-done.11.got_ref = bf16[128,768]{1,0:T(8,128)(2,1)S(1)} collective-permute-done((bf16[128,768]{1,0:T(8,128)(2,1)S(1)}, bf16[128,768]{1,0:T(8,128)(2,1)S(1)}, u32[]{:S(2)}, u32[]{:S(2)}) %collective-permute-start.11) | collective-permute-done | bytes 196640 | tf_op jit(solution)/shard_map/ppermute | solution.py:362
  172.8 0.8 fifth_sum.5
  (32 shorter events, 0.2 us)
Async XLA Ops:
  0.8 1.0 copy-start.10
  1.8 0.7 copy-start.12
  2.5 1.0 copy-start.14
  3.6 0.7 copy-start.15
  4.3 45.6 %copy-start.2 = (bf16[1,2048,768]{2,1,0:T(8,128)(2,1)S(1)}, bf16[1,2048,768]{2,1,0:T(8,128)(2,1)}, u32[]{:S(2)}) copy-start(bf16[1,2048,768]{2,1,0:T(8,128)(2,1)} %param.13) | copy-start | bytes 9437188
  6.0 43.9 %copy-start = (bf16[1,2048,768]{2,1,0:T(8,128)(2,1)S(1)}, bf16[1,2048,768]{2,1,0:T(8,128)(2,1)}, u32[]{:S(2)}) copy-start(bf16[1,2048,768]{2,1,0:T(8,128)(2,1)} %param.11) | copy-start | bytes 9437188
  6.0 43.8 %copy-start.1 = (bf16[1,2048,768]{2,1,0:T(8,128)(2,1)S(1)}, bf16[1,2048,768]{2,1,0:T(8,128)(2,1)}, u32[]{:S(2)}) copy-start(bf16[1,2048,768]{2,1,0:T(8,128)(2,1)} %param.12) | copy-start | bytes 9437188
  54.9 4.4 %copy-start.3 = (bf16[384,768]{1,0:T(8,128)(2,1)}, bf16[384,768]{1,0:T(8,128)(2,1)S(1)}, u32[]{:S(2)}) copy-start(bf16[384,768]{1,0:T(8,128)(2,1)S(1)} %get-tuple-element.62.rhs_ref.d_gate_ref) | copy-start | bytes 1769476
  54.9 4.3 %copy-start.6 = (bf16[384,768]{1,0:T(8,128)(2,1)}, bf16[384,768]{1,0:T(8,128)(2,1)S(1)}, u32[]{:S(2)}) copy-start(bf16[384,768]{1,0:T(8,128)(2,1)S(1)} %get-tuple-element.61.hidden_ref.rhs_ref) | copy-start | bytes 1769476
  54.9 4.3 %copy-start.8 = (bf16[384,768]{1,0:T(8,128)(2,1)}, bf16[384,768]{1,0:T(8,128)(2,1)S(1)}, u32[]{:S(2)}) copy-start(bf16[384,768]{1,0:T(8,128)(2,1)S(1)} %get-tuple-element.63.d_up_ref.rhs_ref) | copy-start | bytes 1769476
  57.8 20.7 %collective-permute-start = (bf16[1024,768]{1,0:T(8,128)(2,1)}, bf16[1024,768]{1,0:T(8,128)(2,1)}, u32[]{:S(2)}, u32[]{:S(2)}) collective-permute-start(bf16[1024,768]{1,0:T(8,128)(2,1)} %get-tuple-element.69), channel_id=1, source_target_pairs={{0,64},{1,193},{2,66},{3,195},{4,68},{5,197},{6,70},{7,199},{8,72}... | collective-permute-start | bytes 4718600 | tf_op jit(solution)/shard_map/ppermute | solution.py:362
  63.9 1.7 copy-start.5
  65.6 83.8 %all-to-all-start.1 = ((bf16[16,24,4096]{2,1,0:T(8,128)(2,1)}), bf16[16,24,4096]{2,1,0:T(8,128)(2,1)}, u32[]{:S(2)}, u32[]{:S(2)}) async-start(bf16[16,24,4096]{2,1,0:T(8,128)(2,1)} %bitcast.32), calls=%async_computation.1 | async-start | bytes 6291456 | tf_op jit(solution)/shard_map/all_to_all | solution.py:358
  71.1 1.1 copy-start.9
  72.1 3.5 %copy-start.4 = (bf16[384,768]{1,0:T(8,128)(2,1)S(1)}, bf16[384,768]{1,0:T(8,128)(2,1)}, u32[]{:S(2)}) copy-start(bf16[384,768]{1,0:T(8,128)(2,1)} %copy-done.3) | copy-start | bytes 1769476
  77.5 28.9 %collective-permute-start.2 = (bf16[1024,768]{1,0:T(8,128)(2,1)S(1)}, bf16[1024,768]{1,0:T(8,128)(2,1)S(1)}, u32[]{:S(2)}, u32[]{:S(2)}) collective-permute-start(bf16[1024,768]{1,0:T(8,128)(2,1)S(1)} %get-tuple-element.75), channel_id=1, source_target_pairs={{0,64},{1,193},{2,66},{3,195},{4,68},{5,197},{6,70},{7,199},{8,72}... | collective-permute-start | bytes 4718600 | tf_op jit(solution)/shard_map/ppermute | solution.py:362
  78.5 4.6 %copy-start.7 = (bf16[384,768]{1,0:T(8,128)(2,1)S(1)}, bf16[384,768]{1,0:T(8,128)(2,1)}, u32[]{:S(2)}) copy-start(bf16[384,768]{1,0:T(8,128)(2,1)} %copy-done.6) | copy-start | bytes 1769476
  80.3 21.8 %collective-permute-start.3 = (bf16[512,768]{1,0:T(8,128)(2,1)S(1)}, bf16[512,768]{1,0:T(8,128)(2,1)S(1)}, u32[]{:S(2)}, u32[]{:S(2)}) collective-permute-start(bf16[512,768]{1,0:T(8,128)(2,1)S(1)} %get-tuple-element.77), channel_id=1, source_target_pairs={{0,192},{1,65},{2,194},{3,67},{4,196},{5,69},{6,198},{7,71},{8,200... | collective-permute-start | bytes 2359304 | tf_op jit(solution)/shard_map/ppermute | solution.py:362
  86.6 46.2 %collective-permute-start.1 = (bf16[1024,768]{1,0:T(8,128)(2,1)S(1)}, bf16[1024,768]{1,0:T(8,128)(2,1)S(1)}, u32[]{:S(2)}, u32[]{:S(2)}) collective-permute-start(bf16[1024,768]{1,0:T(8,128)(2,1)S(1)} %get-tuple-element.73), channel_id=1, source_target_pairs={{0,64},{1,193},{2,66},{3,195},{4,68},{5,197},{6,70},{7,199},{8,72}... | collective-permute-start | bytes 4718600 | tf_op jit(solution)/shard_map/ppermute | solution.py:362
  102.8 16.0 %collective-permute-start.5 = (bf16[256,768]{1,0:T(8,128)(2,1)S(1)}, bf16[256,768]{1,0:T(8,128)(2,1)S(1)}, u32[]{:S(2)}, u32[]{:S(2)}) collective-permute-start(bf16[256,768]{1,0:T(8,128)(2,1)S(1)} %get-tuple-element.83), channel_id=1, source_target_pairs={{0,16},{1,49},{2,18},{3,51},{4,20},{5,53},{6,22},{7,55},{8,24},{9,... | collective-permute-start | bytes 1179656 | tf_op jit(solution)/shard_map/ppermute | solution.py:362
  106.8 21.8 %collective-permute-start.4 = (bf16[512,768]{1,0:T(8,128)(2,1)S(1)}, bf16[512,768]{1,0:T(8,128)(2,1)S(1)}, u32[]{:S(2)}, u32[]{:S(2)}) collective-permute-start(bf16[512,768]{1,0:T(8,128)(2,1)S(1)} %get-tuple-element.81), channel_id=1, source_target_pairs={{0,192},{1,65},{2,194},{3,67},{4,196},{5,69},{6,198},{7,71},{8,200... | collective-permute-start | bytes 2359304 | tf_op jit(solution)/shard_map/ppermute | solution.py:362
  118.9 16.4 %collective-permute-start.8 = (bf16[128,768]{1,0:T(8,128)(2,1)S(1)}, bf16[128,768]{1,0:T(8,128)(2,1)S(1)}, u32[]{:S(2)}, u32[]{:S(2)}) collective-permute-start(bf16[128,768]{1,0:T(8,128)(2,1)S(1)} %get-tuple-element.92), channel_id=1, source_target_pairs={{0,48},{1,17},{2,50},{3,19},{4,52},{5,21},{6,54},{7,23},{8,56},{9,... | collective-permute-start | bytes 589832 | tf_op jit(solution)/shard_map/ppermute | solution.py:362
  129.3 12.8 %collective-permute-start.7 = (bf16[256,768]{1,0:T(8,128)(2,1)S(1)}, bf16[256,768]{1,0:T(8,128)(2,1)S(1)}, u32[]{:S(2)}, u32[]{:S(2)}) collective-permute-start(bf16[256,768]{1,0:T(8,128)(2,1)S(1)} %get-tuple-element.90), channel_id=1, source_target_pairs={{0,16},{1,49},{2,18},{3,51},{4,20},{5,53},{6,22},{7,55},{8,24},{9,... | collective-permute-start | bytes 1179656 | tf_op jit(solution)/shard_map/ppermute | solution.py:362
  133.2 14.4 %collective-permute-start.6 = (bf16[512,768]{1,0:T(8,128)(2,1)S(1)}, bf16[512,768]{1,0:T(8,128)(2,1)S(1)}, u32[]{:S(2)}, u32[]{:S(2)}) collective-permute-start(bf16[512,768]{1,0:T(8,128)(2,1)S(1)} %get-tuple-element.88), channel_id=1, source_target_pairs={{0,192},{1,65},{2,194},{3,67},{4,196},{5,69},{6,198},{7,71},{8,200... | collective-permute-start | bytes 2359304 | tf_op jit(solution)/shard_map/ppermute | solution.py:362
  142.1 17.3 %collective-permute-start.9 = (bf16[128,768]{1,0:T(8,128)(2,1)S(1)}, bf16[128,768]{1,0:T(8,128)(2,1)S(1)}, u32[]{:S(2)}, u32[]{:S(2)}) collective-permute-start(bf16[128,768]{1,0:T(8,128)(2,1)S(1)} %get-tuple-element.102), channel_id=1, source_target_pairs={{0,48},{1,17},{2,50},{3,19},{4,52},{5,21},{6,54},{7,23},{8,56},{9,... | collective-permute-start | bytes 589832 | tf_op jit(solution)/shard_map/ppermute | solution.py:362
  147.6 1.8 %copy-start.11 = (bf16[128,2048]{1,0:T(8,128)(2,1)S(1)}, bf16[128,2048]{1,0:T(8,128)(2,1)}, u32[]{:S(2)}) copy-start(bf16[128,2048]{1,0:T(8,128)(2,1)} %grads_ref.3) | copy-start | bytes 1572868
  147.6 1.8 %copy-start.13 = (f32[128,6]{0,1:T(8,128)S(1)}, f32[128,6]{0,1:T(8,128)}, u32[]{:S(2)}) copy-start(f32[128,6]{0,1:T(8,128)} %param.10) | copy-start | bytes 9220
  148.4 14.5 %collective-permute-start.10 = (bf16[256,768]{1,0:T(8,128)(2,1)S(1)}, bf16[256,768]{1,0:T(8,128)(2,1)S(1)}, u32[]{:S(2)}, u32[]{:S(2)}) collective-permute-start(bf16[256,768]{1,0:T(8,128)(2,1)S(1)} %get-tuple-element.106), channel_id=1, source_target_pairs={{0,16},{1,49},{2,18},{3,51},{4,20},{5,53},{6,22},{7,55},{8,24},{9,... | collective-permute-start | bytes 1179656 | tf_op jit(solution)/shard_map/ppermute | solution.py:362
  162.9 9.9 %collective-permute-start.11 = (bf16[128,768]{1,0:T(8,128)(2,1)S(1)}, bf16[128,768]{1,0:T(8,128)(2,1)S(1)}, u32[]{:S(2)}, u32[]{:S(2)}) collective-permute-start(bf16[128,768]{1,0:T(8,128)(2,1)S(1)} %get-tuple-element.109), channel_id=1, source_target_pairs={{0,48},{1,17},{2,50},{3,19},{4,52},{5,21},{6,54},{7,23},{8,56},{9,... | collective-permute-start | bytes 589832 | tf_op jit(solution)/shard_map/ppermute | solution.py:362

commit v4 on v3

--- a/solution.py
+++ b/solution.py
@@ -32,8 +32,8 @@
     "fourth gate",
     "third up",
     "second down",
+    "fourth up",
     "fifth gate",
-    "fourth up",
     "third down",
     "run combine",
     "fifth up",

time: 174 us -> 175 us (level)
  no operation moved by 1% of the time
where the time goes in v4:
time: 175 us; the launch traced here: 174 us
  waiting for transfers between devices  57.1 us (33%)
  blocking collectives  43.8 us (25%)
  Pallas kernels  34.8 us (20%)
  starting transfers between devices  31 us (18%)
  local copies, waits for them, and re-layouts  6.32 us (4%)
    ppermute x12, waiting for transfers between devices, send_on(): return lax.ppermute(array, ALL, pairs_of(axis, stage))  57.1 us
    all_to_all x1, blocking collectives, exchange(): lax.all_to_all(buffer, 'expert', split_axis=0, concat_axis=0, tiled=True)  43.8 us
    ppermute x12, starting transfers between devices, send_on(): return lax.ppermute(array, ALL, pairs_of(axis, stage))  25.5 us
    pallas_call x4, Pallas kernels, partial(): pl.pallas_call(partial_kernel, grid_spec=pltpu.PrefetchScalarGridSpec(num...  11.6 us
    unnamed x32, local copies, waits for them, and re-layouts  6.23 us
    all_to_all x1, starting transfers between devices, exchange(): lax.all_to_all(buffer, 'expert', split_axis=0, concat_axis=0, tiled=True)  5.45 us
    pallas_call x1, Pallas kernels, hidden_pass(): pl.pallas_call(hidden_kernel, grid=(FF // tile,), in_specs=[pl.BlockSpec(...  5.04 us
    pallas_call x1, Pallas kernels, back_pass(): pl.pallas_call(back_kernel, grid=(D // OUT_TILE,), in_specs=[act, act, ac...  4.65 us
  transfers between devices with their start and end apart: 13, of which 9 were waited for; matrix products, arithmetic and copies ran while one was open for 0% of the time, Pallas kernels for 14%

profile of v4, /device:TPU:32, one launch (start us, length us, event | category | flops | bytes accessed | tf_op | source)
XLA Modules:
  0.0 174.0 jit_solution(14517008085759042893)
XLA Ops:
  0.8 1.0 copy-done.10
  1.8 0.7 copy-done.12
  2.5 1.0 copy-done.14
  3.6 0.7 copy-done.15
  4.3 1.7 place_rows.1
  6.0 43.8 %all_to_all.10 = bf16[16,24,4096]{2,1,0:T(8,128)(2,1)S(1)} all-to-all(bf16[16,24,4096]{2,1,0:T(8,128)(2,1)S(1)} %bitcast.33), channel_id=1, replica_groups=mesh['dp'=16,'expert'=16] {'expert'}, dimensions={0} | all-to-all | bytes 6291456 | tf_op jit(solution)/shard_map/all_to_all | solution.py:358
  49.9 5.0 %hidden_pass.1 = (bf16[384,768]{1,0:T(8,128)(2,1)S(1)}, bf16[384,768]{1,0:T(8,128)(2,1)S(1)}, bf16[384,768]{1,0:T(8,128)(2,1)S(1)}) custom-call(bf16[384,4096]{1,0:T(8,128)(2,1)S(1)} %bitcast.21, bf16[2048,768]{1,0:T(8,128)(2,1)S(1)} %bitcast.26, bf16[2048,768]{1,0:T(8,128)(2,1)S(1)} %bitcast.28, bf16[2048,768]{1,0:T(8,128)(2,1)S(1)} %bitcast.30), custom_call_target="tpu_custom_call" | custom-call | flops 1 | bytes 1 | tf_op jit(solution)/shard_map/hidden_pass/pallas_call | solution.py:134
  54.9 2.8 %partial.4 = (bf16[1024,768]{1,0:T(8,128)(2,1)}, s32[8,128]{1,0:T(8,128)S(1)}) custom-call(s32[8]{0:T(128)S(1)} %stack.35.at_ref, bf16[384,4096]{1,0:T(8,128)(2,1)S(1)} %bitcast.22, bf16[384,768]{1,0:T(8,128)(2,1)S(1)} %get-tuple-element.62.rhs_ref.d_gate_ref, s32[6,128]{1,0:T(8,128)S(1)} %get-tuple-element.59.after_ref.target_ref), custom_call_target="tpu_custom_call" | custom-call | flops 1 | bytes 1 | tf_op jit(solution)/shard_map/partial/pallas_call | solution.py:207
  57.8 1.5 collective-permute-start
  59.3 4.6 %back_pass.1 = (bf16[384,4096]{1,0:T(8,128)(2,1)S(1)}, s32[8,128]{1,0:T(8,128)S(1)}) custom-call(bf16[384,768]{1,0:T(8,128)(2,1)S(1)} %get-tuple-element.61.hidden_ref.rhs_ref, bf16[384,768]{1,0:T(8,128)(2,1)S(1)} %get-tuple-element.62.rhs_ref.d_gate_ref, bf16[384,768]{1,0:T(8,128)(2,1)S(1)} %get-tuple-element.63.d_up_ref.rhs_ref, ...), custom_call_target="tpu_custom_call" | custom-call | flops 1 | bytes 1 | tf_op jit(solution)/shard_map/back_pass/pallas_call | solution.py:173
  63.9 1.7 copy-done.5
  65.6 5.5 %all-to-all-start.1 = ((bf16[16,24,4096]{2,1,0:T(8,128)(2,1)}), bf16[16,24,4096]{2,1,0:T(8,128)(2,1)}, u32[]{:S(2)}, u32[]{:S(2)}) async-start(bf16[16,24,4096]{2,1,0:T(8,128)(2,1)} %bitcast.32), calls=%async_computation.1 | async-start | bytes 6291456 | tf_op jit(solution)/shard_map/all_to_all | solution.py:358
  71.1 1.1 copy-done.9
  72.1 3.5 %partial.5 = (bf16[1024,768]{1,0:T(8,128)(2,1)S(1)}, bf16[1024,768]{1,0:T(8,128)(2,1)S(1)}, s32[8,128]{1,0:T(8,128)S(1)}) custom-call(s32[8]{0:T(128)S(1)} %stack.35.at_ref, bf16[384,4096]{1,0:T(8,128)(2,1)S(1)} %bitcast.23, bf16[384,768]{1,0:T(8,128)(2,1)S(1)} %copy-done.9, s32[8,128]{1,0:T(8,128)S(1)} %get-tuple-element.66.after_ref), custom_call_target="tpu_custom_call" | custom-call | flops 1 | bytes 1 | tf_op jit(solution)/shard_map/partial/pallas_call | solution.py:207
  75.6 1.9 %partial.6 = (bf16[1024,768]{1,0:T(8,128)(2,1)S(1)}, s32[8,128]{1,0:T(8,128)S(1)}) custom-call(s32[8]{0:T(128)S(1)} %stack.35.at_ref, bf16[384,4096]{1,0:T(8,128)(2,1)S(1)} %bitcast.24, bf16[384,768]{1,0:T(8,128)(2,1)S(1)} %copy-done.4, s32[8,128]{1,0:T(8,128)S(1)} %get-tuple-element.67.after_ref), custom_call_target="tpu_custom_call" | custom-call | flops 1 | bytes 1 | tf_op jit(solution)/shard_map/partial/pallas_call | solution.py:207
  77.5 0.7 collective-permute-start.2
  78.1 0.3 collective-permute-done.got_next_ref.got_own_ref
  78.5 1.8 %split_sum.6 = (bf16[512,768]{1,0:T(8,128)(2,1)S(1)}, bf16[512,768]{1,0:T(8,128)(2,1)S(1)}, s32[8,128]{1,0:T(8,128)S(1)}) custom-call(bf16[1024,768]{1,0:T(8,128)(2,1)S(1)} %get-tuple-element.68.own_ref.next_ref, bf16[1024,768]{1,0:T(8,128)(2,1)S(1)} %get-tuple-element.68.own_ref.next_ref, bf16[1024,768]{1,0:T(8,128)(2,1)} %collective-permute-done.got_next_ref.got_own_ref, ...), custom_call_target="tpu_custom_call" | custom-call | flops 6000000000 | bytes 1 | tf_op jit(solution)/shard_map/split_sum/pallas_call | solution.py:239
  80.3 2.8 %collective-permute-start.3 = (bf16[512,768]{1,0:T(8,128)(2,1)S(1)}, bf16[512,768]{1,0:T(8,128)(2,1)S(1)}, u32[]{:S(2)}, u32[]{:S(2)}) collective-permute-start(bf16[512,768]{1,0:T(8,128)(2,1)S(1)} %get-tuple-element.77), channel_id=1, source_target_pairs={{0,192},{1,65},{2,194},{3,67},{4,196},{5,69},{6,198},{7,71},{8,200... | collective-permute-start | bytes 2359304 | tf_op jit(solution)/shard_map/ppermute | solution.py:362
  83.1 3.5 %partial.7 = (bf16[1024,768]{1,0:T(8,128)(2,1)S(1)}, bf16[1024,768]{1,0:T(8,128)(2,1)S(1)}, s32[8,128]{1,0:T(8,128)S(1)}) custom-call(s32[8]{0:T(128)S(1)} %stack.35.at_ref, bf16[384,4096]{1,0:T(8,128)(2,1)S(1)} %bitcast.25, bf16[384,768]{1,0:T(8,128)(2,1)S(1)} %copy-done.7, s32[8,128]{1,0:T(8,128)S(1)} %get-tuple-element.71.after_ref), custom_call_target="tpu_custom_call" | custom-call | flops 1 | bytes 1 | tf_op jit(solution)/shard_map/partial/pallas_call | solution.py:207
  86.6 0.3 collective-permute-start.1
  86.9 15.1 %collective-permute-done.3.got_ref = bf16[512,768]{1,0:T(8,128)(2,1)S(1)} collective-permute-done((bf16[512,768]{1,0:T(8,128)(2,1)S(1)}, bf16[512,768]{1,0:T(8,128)(2,1)S(1)}, u32[]{:S(2)}, u32[]{:S(2)}) %collective-permute-start.3) | collective-permute-done | bytes 786464 | tf_op jit(solution)/shard_map/ppermute | solution.py:362
  102.1 0.7 third_sum.3
  102.8 3.4 %collective-permute-start.5 = (bf16[256,768]{1,0:T(8,128)(2,1)S(1)}, bf16[256,768]{1,0:T(8,128)(2,1)S(1)}, u32[]{:S(2)}, u32[]{:S(2)}) collective-permute-start(bf16[256,768]{1,0:T(8,128)(2,1)S(1)} %get-tuple-element.83), channel_id=1, source_target_pairs={{0,16},{1,49},{2,18},{3,51},{4,20},{5,53},{6,22},{7,55},{8,24},{9,... | collective-permute-start | bytes 1179656 | tf_op jit(solution)/shard_map/ppermute | solution.py:362
  106.2 0.3 collective-permute-done.2.got_next_ref.got_own_ref
  106.4 0.4 split_sum.7
  106.8 2.6 %collective-permute-start.4 = (bf16[512,768]{1,0:T(8,128)(2,1)S(1)}, bf16[512,768]{1,0:T(8,128)(2,1)S(1)}, u32[]{:S(2)}, u32[]{:S(2)}) collective-permute-start(bf16[512,768]{1,0:T(8,128)(2,1)S(1)} %get-tuple-element.81), channel_id=1, source_target_pairs={{0,192},{1,65},{2,194},{3,67},{4,196},{5,69},{6,198},{7,71},{8,200... | collective-permute-start | bytes 2359304 | tf_op jit(solution)/shard_map/ppermute | solution.py:362
  109.4 9.5 %collective-permute-done.5.got_next_ref.got_own_ref = bf16[256,768]{1,0:T(8,128)(2,1)S(1)} collective-permute-done((bf16[256,768]{1,0:T(8,128)(2,1)S(1)}, bf16[256,768]{1,0:T(8,128)(2,1)S(1)}, u32[]{:S(2)}, u32[]{:S(2)}) %collective-permute-start.5) | collective-permute-done | bytes 393248 | tf_op jit(solution)/shard_map/ppermute | solution.py:362
  118.8 0.1 split_sum.8
  118.9 1.8 %collective-permute-start.7 = (bf16[128,768]{1,0:T(8,128)(2,1)S(1)}, bf16[128,768]{1,0:T(8,128)(2,1)S(1)}, u32[]{:S(2)}, u32[]{:S(2)}) collective-permute-start(bf16[128,768]{1,0:T(8,128)(2,1)S(1)} %get-tuple-element.90), channel_id=1, source_target_pairs={{0,48},{1,17},{2,50},{3,19},{4,52},{5,21},{6,54},{7,23},{8,56},{9,... | collective-permute-start | bytes 589832 | tf_op jit(solution)/shard_map/ppermute | solution.py:362
  120.7 7.9 %collective-permute-done.4.got_ref = bf16[512,768]{1,0:T(8,128)(2,1)S(1)} collective-permute-done((bf16[512,768]{1,0:T(8,128)(2,1)S(1)}, bf16[512,768]{1,0:T(8,128)(2,1)S(1)}, u32[]{:S(2)}, u32[]{:S(2)}) %collective-permute-start.4) | collective-permute-done | bytes 786464 | tf_op jit(solution)/shard_map/ppermute | solution.py:362
  128.6 0.7 third_sum.4
  129.3 3.5 %collective-permute-start.8 = (bf16[256,768]{1,0:T(8,128)(2,1)S(1)}, bf16[256,768]{1,0:T(8,128)(2,1)S(1)}, u32[]{:S(2)}, u32[]{:S(2)}) collective-permute-start(bf16[256,768]{1,0:T(8,128)(2,1)S(1)} %get-tuple-element.92), channel_id=1, source_target_pairs={{0,16},{1,49},{2,18},{3,51},{4,20},{5,53},{6,22},{7,55},{8,24},{9,... | collective-permute-start | bytes 1179656 | tf_op jit(solution)/shard_map/ppermute | solution.py:362
  132.8 0.4 split_sum.9
  133.2 2.2 %collective-permute-start.6 = (bf16[512,768]{1,0:T(8,128)(2,1)S(1)}, bf16[512,768]{1,0:T(8,128)(2,1)S(1)}, u32[]{:S(2)}, u32[]{:S(2)}) collective-permute-start(bf16[512,768]{1,0:T(8,128)(2,1)S(1)} %get-tuple-element.88), channel_id=1, source_target_pairs={{0,192},{1,65},{2,194},{3,67},{4,196},{5,69},{6,198},{7,71},{8,200... | collective-permute-start | bytes 2359304 | tf_op jit(solution)/shard_map/ppermute | solution.py:362
  135.4 6.7 %collective-permute-done.8.got_next_ref.got_own_ref = bf16[256,768]{1,0:T(8,128)(2,1)S(1)} collective-permute-done((bf16[256,768]{1,0:T(8,128)(2,1)S(1)}, bf16[256,768]{1,0:T(8,128)(2,1)S(1)}, u32[]{:S(2)}, u32[]{:S(2)}) %collective-permute-start.8) | collective-permute-done | bytes 393248 | tf_op jit(solution)/shard_map/ppermute | solution.py:362
  142.1 5.5 %collective-permute-start.9 = (bf16[128,768]{1,0:T(8,128)(2,1)S(1)}, bf16[128,768]{1,0:T(8,128)(2,1)S(1)}, u32[]{:S(2)}, u32[]{:S(2)}) collective-permute-start(bf16[128,768]{1,0:T(8,128)(2,1)S(1)} %get-tuple-element.102), channel_id=1, source_target_pairs={{0,48},{1,17},{2,50},{3,19},{4,52},{5,21},{6,54},{7,23},{8,56},{9,... | collective-permute-start | bytes 589832 | tf_op jit(solution)/shard_map/ppermute | solution.py:362
  147.6 0.8 fifth_sum.3
  148.4 0.7 third_sum.5
  149.2 0.7 collective-permute-start.10
  149.9 4.4 %combine_rows.1 = (bf16[128,2048]{1,0:T(8,128)(2,1)}, bf16[128,2048]{1,0:T(8,128)(2,1)}, f32[6,128]{1,0:T(8,128)}, s32[8,128]{1,0:T(8,128)S(1)}) custom-call(s32[6,128]{1,0:T(8,128)S(1)} %get-tuple-element.59.after_ref.target_ref, f32[6,128]{1,0:T(8,128)S(1)} %bitcast.35, bf16[384,4096]{1,0:T(8,128)(2,1)} %bitcast.16.back_ref, ...), custom_call_target="tpu_custom_call" | custom-call | flops 1 | bytes 1 | tf_op jit(solution)/shard_map/combine_rows/pallas_call | solution.py:327
  154.3 5.2 %collective-permute-done.9.got_ref = bf16[128,768]{1,0:T(8,128)(2,1)S(1)} collective-permute-done((bf16[128,768]{1,0:T(8,128)(2,1)S(1)}, bf16[128,768]{1,0:T(8,128)(2,1)S(1)}, u32[]{:S(2)}, u32[]{:S(2)}) %collective-permute-start.9) | collective-permute-done | bytes 196640 | tf_op jit(solution)/shard_map/ppermute | solution.py:362
  159.5 0.8 fifth_sum.4
  160.3 3.4 %collective-permute-done.10.got_next_ref.got_own_ref = bf16[256,768]{1,0:T(8,128)(2,1)S(1)} collective-permute-done((bf16[256,768]{1,0:T(8,128)(2,1)S(1)}, bf16[256,768]{1,0:T(8,128)(2,1)S(1)}, u32[]{:S(2)}, u32[]{:S(2)}) %collective-permute-start.10) | collective-permute-done | bytes 393248 | tf_op jit(solution)/shard_map/ppermute | solution.py:362
  163.7 0.1 split_sum.11
  163.8 0.6 collective-permute-start.11
  164.3 8.8 %collective-permute-done.11.got_ref = bf16[128,768]{1,0:T(8,128)(2,1)S(1)} collective-permute-done((bf16[128,768]{1,0:T(8,128)(2,1)S(1)}, bf16[128,768]{1,0:T(8,128)(2,1)S(1)}, u32[]{:S(2)}, u32[]{:S(2)}) %collective-permute-start.11) | collective-permute-done | bytes 196640 | tf_op jit(solution)/shard_map/ppermute | solution.py:362
  173.2 0.8 fifth_sum.5
  (32 shorter events, 0.2 us)
Async XLA Ops:
  0.8 1.0 copy-start.10
  1.8 0.7 copy-start.12
  2.5 1.0 copy-start.14
  3.6 0.7 copy-start.15
  4.3 45.6 %copy-start.2 = (bf16[1,2048,768]{2,1,0:T(8,128)(2,1)S(1)}, bf16[1,2048,768]{2,1,0:T(8,128)(2,1)}, u32[]{:S(2)}) copy-start(bf16[1,2048,768]{2,1,0:T(8,128)(2,1)} %param.13) | copy-start | bytes 9437188
  6.0 43.9 %copy-start = (bf16[1,2048,768]{2,1,0:T(8,128)(2,1)S(1)}, bf16[1,2048,768]{2,1,0:T(8,128)(2,1)}, u32[]{:S(2)}) copy-start(bf16[1,2048,768]{2,1,0:T(8,128)(2,1)} %param.11) | copy-start | bytes 9437188
  6.0 43.8 %copy-start.1 = (bf16[1,2048,768]{2,1,0:T(8,128)(2,1)S(1)}, bf16[1,2048,768]{2,1,0:T(8,128)(2,1)}, u32[]{:S(2)}) copy-start(bf16[1,2048,768]{2,1,0:T(8,128)(2,1)} %param.12) | copy-start | bytes 9437188
  54.9 4.4 %copy-start.3 = (bf16[384,768]{1,0:T(8,128)(2,1)}, bf16[384,768]{1,0:T(8,128)(2,1)S(1)}, u32[]{:S(2)}) copy-start(bf16[384,768]{1,0:T(8,128)(2,1)S(1)} %get-tuple-element.62.rhs_ref.d_gate_ref) | copy-start | bytes 1769476
  54.9 4.3 %copy-start.6 = (bf16[384,768]{1,0:T(8,128)(2,1)}, bf16[384,768]{1,0:T(8,128)(2,1)S(1)}, u32[]{:S(2)}) copy-start(bf16[384,768]{1,0:T(8,128)(2,1)S(1)} %get-tuple-element.61.hidden_ref.rhs_ref) | copy-start | bytes 1769476
  54.9 4.3 %copy-start.8 = (bf16[384,768]{1,0:T(8,128)(2,1)}, bf16[384,768]{1,0:T(8,128)(2,1)S(1)}, u32[]{:S(2)}) copy-start(bf16[384,768]{1,0:T(8,128)(2,1)S(1)} %get-tuple-element.63.d_up_ref.rhs_ref) | copy-start | bytes 1769476
  57.8 20.7 %collective-permute-start = (bf16[1024,768]{1,0:T(8,128)(2,1)}, bf16[1024,768]{1,0:T(8,128)(2,1)}, u32[]{:S(2)}, u32[]{:S(2)}) collective-permute-start(bf16[1024,768]{1,0:T(8,128)(2,1)} %get-tuple-element.69), channel_id=1, source_target_pairs={{0,64},{1,193},{2,66},{3,195},{4,68},{5,197},{6,70},{7,199},{8,72}... | collective-permute-start | bytes 4718600 | tf_op jit(solution)/shard_map/ppermute | solution.py:362
  63.9 1.7 copy-start.5
  65.6 84.3 %all-to-all-start.1 = ((bf16[16,24,4096]{2,1,0:T(8,128)(2,1)}), bf16[16,24,4096]{2,1,0:T(8,128)(2,1)}, u32[]{:S(2)}, u32[]{:S(2)}) async-start(bf16[16,24,4096]{2,1,0:T(8,128)(2,1)} %bitcast.32), calls=%async_computation.1 | async-start | bytes 6291456 | tf_op jit(solution)/shard_map/all_to_all | solution.py:358
  71.1 1.1 copy-start.9
  72.1 3.5 %copy-start.4 = (bf16[384,768]{1,0:T(8,128)(2,1)S(1)}, bf16[384,768]{1,0:T(8,128)(2,1)}, u32[]{:S(2)}) copy-start(bf16[384,768]{1,0:T(8,128)(2,1)} %copy-done.3) | copy-start | bytes 1769476
  77.5 28.9 %collective-permute-start.2 = (bf16[1024,768]{1,0:T(8,128)(2,1)S(1)}, bf16[1024,768]{1,0:T(8,128)(2,1)S(1)}, u32[]{:S(2)}, u32[]{:S(2)}) collective-permute-start(bf16[1024,768]{1,0:T(8,128)(2,1)S(1)} %get-tuple-element.75), channel_id=1, source_target_pairs={{0,64},{1,193},{2,66},{3,195},{4,68},{5,197},{6,70},{7,199},{8,72}... | collective-permute-start | bytes 4718600 | tf_op jit(solution)/shard_map/ppermute | solution.py:362
  78.5 4.6 %copy-start.7 = (bf16[384,768]{1,0:T(8,128)(2,1)S(1)}, bf16[384,768]{1,0:T(8,128)(2,1)}, u32[]{:S(2)}) copy-start(bf16[384,768]{1,0:T(8,128)(2,1)} %copy-done.6) | copy-start | bytes 1769476
  80.3 21.8 %collective-permute-start.3 = (bf16[512,768]{1,0:T(8,128)(2,1)S(1)}, bf16[512,768]{1,0:T(8,128)(2,1)S(1)}, u32[]{:S(2)}, u32[]{:S(2)}) collective-permute-start(bf16[512,768]{1,0:T(8,128)(2,1)S(1)} %get-tuple-element.77), channel_id=1, source_target_pairs={{0,192},{1,65},{2,194},{3,67},{4,196},{5,69},{6,198},{7,71},{8,200... | collective-permute-start | bytes 2359304 | tf_op jit(solution)/shard_map/ppermute | solution.py:362
  86.6 46.2 %collective-permute-start.1 = (bf16[1024,768]{1,0:T(8,128)(2,1)S(1)}, bf16[1024,768]{1,0:T(8,128)(2,1)S(1)}, u32[]{:S(2)}, u32[]{:S(2)}) collective-permute-start(bf16[1024,768]{1,0:T(8,128)(2,1)S(1)} %get-tuple-element.73), channel_id=1, source_target_pairs={{0,64},{1,193},{2,66},{3,195},{4,68},{5,197},{6,70},{7,199},{8,72}... | collective-permute-start | bytes 4718600 | tf_op jit(solution)/shard_map/ppermute | solution.py:362
  102.8 16.0 %collective-permute-start.5 = (bf16[256,768]{1,0:T(8,128)(2,1)S(1)}, bf16[256,768]{1,0:T(8,128)(2,1)S(1)}, u32[]{:S(2)}, u32[]{:S(2)}) collective-permute-start(bf16[256,768]{1,0:T(8,128)(2,1)S(1)} %get-tuple-element.83), channel_id=1, source_target_pairs={{0,16},{1,49},{2,18},{3,51},{4,20},{5,53},{6,22},{7,55},{8,24},{9,... | collective-permute-start | bytes 1179656 | tf_op jit(solution)/shard_map/ppermute | solution.py:362
  106.8 21.8 %collective-permute-start.4 = (bf16[512,768]{1,0:T(8,128)(2,1)S(1)}, bf16[512,768]{1,0:T(8,128)(2,1)S(1)}, u32[]{:S(2)}, u32[]{:S(2)}) collective-permute-start(bf16[512,768]{1,0:T(8,128)(2,1)S(1)} %get-tuple-element.81), channel_id=1, source_target_pairs={{0,192},{1,65},{2,194},{3,67},{4,196},{5,69},{6,198},{7,71},{8,200... | collective-permute-start | bytes 2359304 | tf_op jit(solution)/shard_map/ppermute | solution.py:362
  118.9 28.7 %collective-permute-start.7 = (bf16[128,768]{1,0:T(8,128)(2,1)S(1)}, bf16[128,768]{1,0:T(8,128)(2,1)S(1)}, u32[]{:S(2)}, u32[]{:S(2)}) collective-permute-start(bf16[128,768]{1,0:T(8,128)(2,1)S(1)} %get-tuple-element.90), channel_id=1, source_target_pairs={{0,48},{1,17},{2,50},{3,19},{4,52},{5,21},{6,54},{7,23},{8,56},{9,... | collective-permute-start | bytes 589832 | tf_op jit(solution)/shard_map/ppermute | solution.py:362
  129.3 12.8 %collective-permute-start.8 = (bf16[256,768]{1,0:T(8,128)(2,1)S(1)}, bf16[256,768]{1,0:T(8,128)(2,1)S(1)}, u32[]{:S(2)}, u32[]{:S(2)}) collective-permute-start(bf16[256,768]{1,0:T(8,128)(2,1)S(1)} %get-tuple-element.92), channel_id=1, source_target_pairs={{0,16},{1,49},{2,18},{3,51},{4,20},{5,53},{6,22},{7,55},{8,24},{9,... | collective-permute-start | bytes 1179656 | tf_op jit(solution)/shard_map/ppermute | solution.py:362
  133.2 15.2 %collective-permute-start.6 = (bf16[512,768]{1,0:T(8,128)(2,1)S(1)}, bf16[512,768]{1,0:T(8,128)(2,1)S(1)}, u32[]{:S(2)}, u32[]{:S(2)}) collective-permute-start(bf16[512,768]{1,0:T(8,128)(2,1)S(1)} %get-tuple-element.88), channel_id=1, source_target_pairs={{0,192},{1,65},{2,194},{3,67},{4,196},{5,69},{6,198},{7,71},{8,200... | collective-permute-start | bytes 2359304 | tf_op jit(solution)/shard_map/ppermute | solution.py:362
  142.1 17.3 %collective-permute-start.9 = (bf16[128,768]{1,0:T(8,128)(2,1)S(1)}, bf16[128,768]{1,0:T(8,128)(2,1)S(1)}, u32[]{:S(2)}, u32[]{:S(2)}) collective-permute-start(bf16[128,768]{1,0:T(8,128)(2,1)S(1)} %get-tuple-element.102), channel_id=1, source_target_pairs={{0,48},{1,17},{2,50},{3,19},{4,52},{5,21},{6,54},{7,23},{8,56},{9,... | collective-permute-start | bytes 589832 | tf_op jit(solution)/shard_map/ppermute | solution.py:362
  148.4 1.4 copy-start.11
  148.4 1.4 copy-start.13
  149.2 14.5 %collective-permute-start.10 = (bf16[256,768]{1,0:T(8,128)(2,1)S(1)}, bf16[256,768]{1,0:T(8,128)(2,1)S(1)}, u32[]{:S(2)}, u32[]{:S(2)}) collective-permute-start(bf16[256,768]{1,0:T(8,128)(2,1)S(1)} %get-tuple-element.106), channel_id=1, source_target_pairs={{0,16},{1,49},{2,18},{3,51},{4,20},{5,53},{6,22},{7,55},{8,24},{9,... | collective-permute-start | bytes 1179656 | tf_op jit(solution)/shard_map/ppermute | solution.py:362
  163.8 9.4 %collective-permute-start.11 = (bf16[128,768]{1,0:T(8,128)(2,1)S(1)}, bf16[128,768]{1,0:T(8,128)(2,1)S(1)}, u32[]{:S(2)}, u32[]{:S(2)}) collective-permute-start(bf16[128,768]{1,0:T(8,128)(2,1)S(1)} %get-tuple-element.109), channel_id=1, source_target_pairs={{0,48},{1,17},{2,50},{3,19},{4,52},{5,21},{6,54},{7,23},{8,56},{9,... | collective-permute-start | bytes 589832 | tf_op jit(solution)/shard_map/ppermute | solution.py:362
